TPU v7x, 32 devices: a whole 2x2x4 slice. The times are simulated.
32 devices in a mesh: dp: 16 (over z, y, x), mp: 2 (over core).
Axes of the slice: x: 2, y: 2, z: 4, core: 2. Of those that a mesh axis runs over, the one named last changes fastest.
Arguments:
- tokens: bfloat16 [16, 1024, 1024], P('dp', 'mp'), may hold values from -6 to 6
- memory: bfloat16 [16, 512, 1024], P('dp', 'mp'), may hold values from -6 to 6
- segments: int32 [16, 1024], P('dp'), may hold values from 0 to 8, as said below
- sources: int32 [16, 512], P('dp'), may hold values from 0 to 8, as said below
- gains: float32 [3, 1024], replicated, may hold values from 0.5 to 1.5
- biases: float32 [6, 1024], replicated, may hold values from -1.8 to 1.8
- head_biases: float32 [4, 1024], P(None, 'mp'), may hold values from -1.8 to 1.8
- self_proj: float32 [3, 1024, 1024], P(None, 'dp', 'mp'), may hold values from -0.1875 to 0.1875
- self_out: float32 [1024, 1024], P('mp', 'dp'), may hold values from -0.75 to 0.75
- cross_query: float32 [1024, 1024], P('dp', 'mp'), may hold values from -0.1875 to 0.1875
- cross_kv: float32 [2, 1024, 1024], P(None, 'dp', 'mp'), may hold values from -0.1875 to 0.1875
- cross_out: float32 [1024, 1024], P('mp', 'dp'), may hold values from -0.75 to 0.75
- up_weight: float32 [1024, 8192], P('dp', 'mp'), may hold values from -0.1875 to 0.1875
- up_bias: float32 [8192], P('mp'), may hold values from -1.8 to 1.8
- down_weight: float32 [8192, 1024], P('mp', 'dp'), may hold values from -0.0625 to 0.0625
- cotangent: bfloat16 [16, 1024, 1024], P('dp', 'mp'), may hold values from -6 to 6
Outputs:
- layer_out: bfloat16 [16, 1024, 1024], P('dp', 'mp')
- d_tokens: bfloat16 [16, 1024, 1024], P('dp', 'mp')
- d_memory: bfloat16 [16, 512, 1024], P('dp', 'mp')
- d_gains: float32 [3, 1024], replicated
- d_biases: float32 [6, 1024], replicated
- d_head_biases: float32 [4, 1024], P(None, 'mp')
- d_self_proj: float32 [3, 1024, 1024], P(None, 'dp', 'mp')
- d_self_out: float32 [1024, 1024], P('mp', 'dp')
- d_cross_query: float32 [1024, 1024], P('dp', 'mp')
- d_cross_kv: float32 [2, 1024, 1024], P(None, 'dp', 'mp')
- d_cross_out: float32 [1024, 1024], P('mp', 'dp')
- d_up_weight: float32 [1024, 8192], P('dp', 'mp')
- d_up_bias: float32 [8192], P('mp')
- d_down_weight: float32 [8192, 1024], P('mp', 'dp')
Inputs may be any that keep to these rules, and one draw needn't show every extreme that they name: `segments`: in each sequence the document numbers never fall; documents 1 to 8 are followed by 1 to 128 positions of padding 0 at the end; one document covers the positions from 384 to 639. `sources`: in each memory the source numbers 1 to 8 follow in order, each on one position or more, then 1 to 64 positions of padding 0 at the end.
All inputs are finite; a program needn't handle non-finite values.
Results may differ from a plain program's by a relative error of at most 0.02.
Values may be sent and summed in bfloat16 or wider, within the bound.
No kernel may reach another device: no remote copies, remote signals or barrier semaphores. Data moves between devices by JAX's collectives and lax.ppermute only.
A program may use at most 192 MiB of HBM per device.

v0:
```python
import math

import jax
import jax.numpy as jnp
from jax import lax
from jax.sharding import PartitionSpec as P

HEAD = 64


def shortened(shard):

    def short(part):
        return part.astype(jnp.bfloat16) if part.dtype == jnp.float32 else part

    return jax.tree.map(short, shard)


def normalize(values, gain_row, shift_row):
    average = jnp.mean(values, axis=-1, keepdims=True)
    centred = values - average
    spread = jnp.mean(centred * centred, axis=-1, keepdims=True)
    return centred * lax.rsqrt(spread + 1e-05) * gain_row + shift_row


def gelu_exact(values):
    return jax.nn.gelu(values, approximate=False)


def project(operand, weight):
    return jnp.einsum("srk,kn->srn", operand, weight, preferred_element_type=jnp.float32)


def project_back(grad_rows, weight):
    return jnp.einsum("srn,kn->srk", grad_rows, weight, preferred_element_type=jnp.float32)


def weight_grad(operand, grad_rows):
    return jnp.einsum("srk,srn->kn", operand, grad_rows, preferred_element_type=jnp.float32)


def row_total(grad_rows):
    return jnp.sum(grad_rows.astype(jnp.float32), axis=(0, 1))


def split_heads(values):
    return values.reshape(values.shape[0], values.shape[1], values.shape[2] // HEAD, HEAD)


def merge_heads(values):
    return values.reshape(values.shape[0], values.shape[1], values.shape[2] * values.shape[3])


def widen(values):
    return jax.tree.map(
        lambda part, own: part.astype(own.dtype),
        lax.all_gather(shortened(values), "mp", axis=1, tiled=True),
        values,
    )


def narrow(values):
    return jax.tree.map(
        lambda part: part.astype(jnp.float32),
        lax.psum_scatter(shortened(values), "mp", scatter_dimension=1, tiled=True),
    )


def add_member(summed, part_rows, member):
    current = lax.dynamic_index_in_dim(summed, member, 0, False)
    return lax.dynamic_update_index_in_dim(summed, current + part_rows, member, 0)


def block_inputs(queries, key_rows, value_rows, member, offset, height):
    query_block = lax.dynamic_slice_in_dim(
        lax.dynamic_index_in_dim(queries, member, 0, False), offset, height, 0
    )
    key_block = lax.dynamic_index_in_dim(key_rows, member, 0, False)
    value_block = lax.dynamic_index_in_dim(value_rows, member, 0, False)
    return (query_block, key_block, value_block)


def block_scores(query_block, key_block, allowed):
    scores = jnp.einsum(
        "qhe,khe->hqk", query_block, key_block, preferred_element_type=jnp.float32
    ) * (1.0 / math.sqrt(HEAD))
    return jnp.where(allowed[None], scores, -1e30)


def attend_forward(queries, key_rows, value_rows, allowed_of):
    members, length = (queries.shape[0], queries.shape[1])
    height = min(512, length)
    pieces = length // height

    def one_block(number):
        member = number // pieces
        offset = number % pieces * height
        query_block, key_block, value_block = block_inputs(
            queries, key_rows, value_rows, member, offset, height
        )
        scores = block_scores(query_block, key_block, allowed_of(member, offset, height))
        largest = jnp.max(scores, axis=-1, keepdims=True)
        exponent = jnp.exp(scores - largest)
        summed = jnp.sum(exponent, axis=-1, keepdims=True)
        chance = (exponent / summed).astype(jnp.bfloat16)
        result = jnp.einsum("hqk,khe->qhe", chance, value_block, preferred_element_type=jnp.float32)
        return (result, (largest + jnp.log(summed))[:, :, 0])

    results, log_totals = lax.map(one_block, jnp.arange(members * pieces))
    return (results.reshape(queries.shape), log_totals)


def attend_backward(queries, key_rows, value_rows, grad_rows, log_totals, allowed_of):
    members, length = (queries.shape[0], queries.shape[1])
    height = min(512, length)
    pieces = length // height
    scale = 1.0 / math.sqrt(HEAD)

    def one_block(carry, number):
        key_grad, value_grad = carry
        member = number // pieces
        offset = number % pieces * height
        query_block, key_block, value_block = block_inputs(
            queries, key_rows, value_rows, member, offset, height
        )
        grad_block = lax.dynamic_slice_in_dim(
            lax.dynamic_index_in_dim(grad_rows, member, 0, False), offset, height, 0
        )
        scores = block_scores(query_block, key_block, allowed_of(member, offset, height))
        log_block = lax.dynamic_index_in_dim(log_totals, number, 0, False)
        chance = jnp.exp(scores - log_block[:, :, None])
        rounded = chance.astype(jnp.bfloat16)
        chance_grad = jnp.einsum(
            "qhe,khe->hqk", grad_block, value_block, preferred_element_type=jnp.float32
        )
        value_part = jnp.einsum(
            "hqk,qhe->khe", rounded, grad_block, preferred_element_type=jnp.float32
        )
        score_grad = (
            chance * (chance_grad - jnp.sum(chance * chance_grad, axis=-1, keepdims=True))
        ).astype(jnp.bfloat16)
        query_grad = (
            jnp.einsum("hqk,khe->qhe", score_grad, key_block, preferred_element_type=jnp.float32)
            * scale
        )
        key_part = (
            jnp.einsum("hqk,qhe->khe", score_grad, query_block, preferred_element_type=jnp.float32)
            * scale
        )
        return (
            (add_member(key_grad, key_part, member), add_member(value_grad, value_part, member)),
            query_grad,
        )

    zeros = jnp.zeros(key_rows.shape, jnp.float32)
    (key_grad, value_grad), query_grad = lax.scan(
        one_block, (zeros, zeros), jnp.arange(members * pieces)
    )
    return (query_grad.reshape(queries.shape), key_grad, value_grad)


def per_device(
    tokens,
    memory,
    segments,
    sources,
    gains,
    biases,
    head_biases,
    self_proj,
    self_out,
    cross_query,
    cross_kv,
    cross_out,
    up_weight,
    up_bias,
    down_weight,
    cotangent,
):

    def self_allowed(member, offset, height):
        seg_row = lax.dynamic_index_in_dim(segments, member, 0, False)
        query_seg = lax.dynamic_slice_in_dim(seg_row, offset, height, 0)
        query_pos = offset + jnp.arange(height)
        key_pos = jnp.arange(seg_row.shape[0])
        return (query_seg[:, None] == seg_row[None, :]) & (query_pos[:, None] >= key_pos[None, :])

    def cross_allowed(member, offset, height):
        seg_row = lax.dynamic_index_in_dim(segments, member, 0, False)
        query_seg = lax.dynamic_slice_in_dim(seg_row, offset, height, 0)
        source_row = lax.dynamic_index_in_dim(sources, member, 0, False)
        return query_seg[:, None] == source_row[None, :]

    self_inputs, self_output, cross_queries_w, cross_pairs, cross_output, hidden_in, hidden_out = (
        lax.all_gather(self_proj.astype(jnp.bfloat16), "dp", axis=1, tiled=True),
        lax.all_gather(self_out.astype(jnp.bfloat16), "dp", axis=1, tiled=True),
        lax.all_gather(cross_query.astype(jnp.bfloat16), "dp", axis=0, tiled=True),
        lax.all_gather(cross_kv.astype(jnp.bfloat16), "dp", axis=1, tiled=True),
        lax.all_gather(cross_out.astype(jnp.bfloat16), "dp", axis=1, tiled=True),
        lax.all_gather(up_weight.astype(jnp.bfloat16), "dp", axis=0, tiled=True),
        lax.all_gather(down_weight.astype(jnp.bfloat16), "dp", axis=1, tiled=True),
    )
    inputs_f = tokens.astype(jnp.float32)
    normed_one, norm_back_one = jax.vjp(normalize, inputs_f, gains[0], biases[0])
    whole_one, whole_memory = widen((normed_one.astype(jnp.bfloat16), memory))
    queries = (project(whole_one, self_inputs[0]) + head_biases[0]).astype(jnp.bfloat16)
    key_rows = project(whole_one, self_inputs[1]).astype(jnp.bfloat16)
    value_rows = (project(whole_one, self_inputs[2]) + head_biases[1]).astype(jnp.bfloat16)
    attended_heads, log_self = attend_forward(
        split_heads(queries), split_heads(key_rows), split_heads(value_rows), self_allowed
    )
    attended = merge_heads(attended_heads).astype(jnp.bfloat16)
    after_self = inputs_f + narrow(project(attended, self_output)) + biases[1]
    normed_two, norm_back_two = jax.vjp(normalize, after_self, gains[1], biases[2])
    whole_two = widen(normed_two.astype(jnp.bfloat16))
    cross_queries = (project(whole_two, cross_queries_w) + head_biases[2]).astype(jnp.bfloat16)
    cross_keys = project(whole_memory, cross_pairs[0]).astype(jnp.bfloat16)
    cross_values = (project(whole_memory, cross_pairs[1]) + head_biases[3]).astype(jnp.bfloat16)
    cross_heads, log_cross = attend_forward(
        split_heads(cross_queries),
        split_heads(cross_keys),
        split_heads(cross_values),
        cross_allowed,
    )
    cross_attended = merge_heads(cross_heads).astype(jnp.bfloat16)
    after_cross = after_self + narrow(project(cross_attended, cross_output)) + biases[3]
    normed_three, norm_back_three = jax.vjp(normalize, after_cross, gains[2], biases[4])
    whole_three = widen(normed_three.astype(jnp.bfloat16))
    hidden_pre = project(whole_three, hidden_in) + up_bias
    activated, gelu_back = jax.vjp(gelu_exact, hidden_pre)
    hidden_act = activated.astype(jnp.bfloat16)
    layer_out = (after_cross + narrow(project(hidden_act, hidden_out)) + biases[5]).astype(
        jnp.bfloat16
    )
    grad_out = cotangent.astype(jnp.float32)
    whole_grad = widen(cotangent)
    d_down_weight = weight_grad(hidden_act, whole_grad)
    d_bias_five = row_total(grad_out)
    d_hidden = gelu_back(project_back(whole_grad, hidden_out))[0].astype(jnp.bfloat16)
    d_up_weight = weight_grad(whole_three, d_hidden)
    d_up_bias = row_total(d_hidden)
    d_norm_three = narrow(project_back(d_hidden, hidden_in))
    back_rows, d_gain_two, d_bias_four = norm_back_three(d_norm_three)
    d_cross_res = grad_out + back_rows
    whole_cross_grad = widen(d_cross_res.astype(jnp.bfloat16))
    d_cross_out = weight_grad(cross_attended, whole_cross_grad)
    d_bias_three = row_total(d_cross_res)
    d_cross_att = project_back(whole_cross_grad, cross_output).astype(jnp.bfloat16)
    cq_grad, ck_grad, cv_grad = attend_backward(
        split_heads(cross_queries),
        split_heads(cross_keys),
        split_heads(cross_values),
        split_heads(d_cross_att),
        log_cross,
        cross_allowed,
    )
    cq_grad = merge_heads(cq_grad).astype(jnp.bfloat16)
    ck_grad = merge_heads(ck_grad).astype(jnp.bfloat16)
    cv_grad = merge_heads(cv_grad).astype(jnp.bfloat16)
    d_cross_query = weight_grad(whole_two, cq_grad)
    d_cross_kv = jnp.stack([weight_grad(whole_memory, ck_grad), weight_grad(whole_memory, cv_grad)])
    memory_terms = project_back(ck_grad, cross_pairs[0]) + project_back(cv_grad, cross_pairs[1])
    d_norm_two, memory_grad = narrow((project_back(cq_grad, cross_queries_w), memory_terms))
    d_memory = memory_grad.astype(jnp.bfloat16)
    back_rows, d_gain_one, d_bias_two = norm_back_two(d_norm_two)
    d_self_res = d_cross_res + back_rows
    whole_self_grad = widen(d_self_res.astype(jnp.bfloat16))
    d_self_out = weight_grad(attended, whole_self_grad)
    d_bias_one = row_total(d_self_res)
    d_attended = project_back(whole_self_grad, self_output).astype(jnp.bfloat16)
    q_grad, k_grad, v_grad = attend_backward(
        split_heads(queries),
        split_heads(key_rows),
        split_heads(value_rows),
        split_heads(d_attended),
        log_self,
        self_allowed,
    )
    q_grad = merge_heads(q_grad).astype(jnp.bfloat16)
    k_grad = merge_heads(k_grad).astype(jnp.bfloat16)
    v_grad = merge_heads(v_grad).astype(jnp.bfloat16)
    d_self_proj = jnp.stack(
        [
            weight_grad(whole_one, q_grad),
            weight_grad(whole_one, k_grad),
            weight_grad(whole_one, v_grad),
        ]
    )
    input_terms = (
        project_back(q_grad, self_inputs[0])
        + project_back(k_grad, self_inputs[1])
        + project_back(v_grad, self_inputs[2])
    )
    d_norm_one = narrow(input_terms)
    back_rows, d_gain_zero, d_bias_zero = norm_back_one(d_norm_one)
    d_tokens = (d_self_res + back_rows).astype(jnp.bfloat16)
    d_self_proj, d_self_out, d_cross_query, d_cross_kv, d_cross_out, d_up_weight, d_down_weight = (
        lax.psum_scatter(d_self_proj, "dp", scatter_dimension=1, tiled=True),
        lax.psum_scatter(d_self_out, "dp", scatter_dimension=1, tiled=True),
        lax.psum_scatter(d_cross_query, "dp", scatter_dimension=0, tiled=True),
        lax.psum_scatter(d_cross_kv, "dp", scatter_dimension=1, tiled=True),
        lax.psum_scatter(d_cross_out, "dp", scatter_dimension=1, tiled=True),
        lax.psum_scatter(d_up_weight, "dp", scatter_dimension=0, tiled=True),
        lax.psum_scatter(d_down_weight, "dp", scatter_dimension=1, tiled=True),
    )
    gain_rows = jnp.stack([d_gain_zero, d_gain_one, d_gain_two])
    bias_rows = jnp.stack(
        [d_bias_zero, d_bias_one, d_bias_two, d_bias_three, d_bias_four, d_bias_five]
    )
    d_gains, d_biases = lax.psum((gain_rows, bias_rows), ("dp", "mp"))
    head_rows = jnp.stack(
        [row_total(q_grad), row_total(v_grad), row_total(cq_grad), row_total(cv_grad)]
    )
    d_head_biases, d_up_bias = lax.psum((head_rows, d_up_bias), "dp")
    return (
        layer_out,
        d_tokens,
        d_memory,
        d_gains,
        d_biases,
        d_head_biases,
        d_self_proj,
        d_self_out,
        d_cross_query,
        d_cross_kv,
        d_cross_out,
        d_up_weight,
        d_up_bias,
        d_down_weight,
    )


def solution(mesh):
    in_specs = (
        P("dp", "mp", None),
        P("dp", "mp", None),
        P("dp", None),
        P("dp", None),
        P(),
        P(),
        P(None, "mp"),
        P(None, "dp", "mp"),
        P("mp", "dp"),
        P("dp", "mp"),
        P(None, "dp", "mp"),
        P("mp", "dp"),
        P("dp", "mp"),
        P("mp"),
        P("mp", "dp"),
        P("dp", "mp", None),
    )
    out_specs = (
        P("dp", "mp", None),
        P("dp", "mp", None),
        P("dp", "mp", None),
        P(),
        P(),
        P(None, "mp"),
        P(None, "dp", "mp"),
        P("mp", "dp"),
        P("dp", "mp"),
        P(None, "dp", "mp"),
        P("mp", "dp"),
        P("dp", "mp"),
        P("mp"),
        P("mp", "dp"),
    )
    return jax.shard_map(
        per_device, mesh=mesh, in_specs=in_specs, out_specs=out_specs, check_vma=False
    )
```

profile of v0, /device:TPU:0, one launch (start us, length us, event | category | flops | bytes accessed | tf_op | source)
XLA Modules:
  0.0 2119.6 jit_solution(16234931882781470985)
XLA Ops:
  27.7 72.1 %all-gather.17.cloned.1.call-done = bf16[3,1024,512]{2,1,0:T(8,128)(2,1)} async-done(((bf16[3,64,512]{2,1,0:T(8,128)(2,1)}), bf16[3,1024,512]{2,1,0:T(8,128)(2,1)}) %all-gather.17.cloned.1.call-update) | async-done | bytes 3145744 | tf_op jit(solution)/shard_map/all_gather | solution.py:195
  107.7 34.1 %while.60 = (s32[]{:T(128)}, bf16[2,512,8,64]{1,3,2,0:T(8,128)(2,1)S(1)}, f32[2,8,512]{2,1,0:T(8,128)}, s32[2]{0:T(128)S(1)}, s32[1,1024]{1,0:T(1,128)S(1)}, /*i...) while((s32[]{:T(128)}, ...), condition=%wide.region_5.6_spmd, body=%wide.region_2.5_spmd.sunk | while | flops 1125642752 | bytes 56245044 | solution.py:109
  181.9 65.4 %all-gather.27.cloned.1.call-done = bf16[2,1024,512]{2,1,0:T(8,128)(2,1)} async-done(((bf16[2,64,512]{2,1,0:T(8,128)(2,1)}), bf16[2,1024,512]{2,1,0:T(8,128)(2,1)}) %all-gather.27.cloned.1.call-update) | async-done | bytes 2097168 | tf_op jit(solution)/shard_map/all_gather | solution.py:198
  250.6 54.3 %all-gather.23.cloned.1.call-done = bf16[1024,512]{1,0:T(8,128)(2,1)} async-done(((bf16[64,512]{1,0:T(8,128)(2,1)}), bf16[1024,512]{1,0:T(8,128)(2,1)}) %all-gather.23.cloned.1.call-update) | async-done | bytes 1048592 | tf_op jit(solution)/shard_map/all_gather | solution.py:197
  320.7 18.5 while.61
  343.6 33.1 %all-gather.29.cloned.1.call-done = bf16[512,1024]{0,1:T(8,128)(2,1)} async-done(((bf16[512,64]{0,1:T(8,128)(2,1)}), bf16[512,1024]{0,1:T(8,128)(2,1)}) %all-gather.29.cloned.1.call-update) | async-done | bytes 1048592 | tf_op jit(solution)/shard_map/all_gather | solution.py:199
  396.2 110.7 %all-gather.33.cloned.1.call-done = bf16[1024,4096]{1,0:T(8,128)(2,1)} async-done(((bf16[64,4096]{1,0:T(8,128)(2,1)}), bf16[1024,4096]{1,0:T(8,128)(2,1)}) %all-gather.33.cloned.1.call-update) | async-done | bytes 8388624 | tf_op jit(solution)/shard_map/all_gather | solution.py:200
  517.6 48.4 %multiply_convert_fusion.2 = (bf16[1024,4096]{1,0:T(8,128)(2,1)}, f32[1024,4096]{1,0:T(8,128)}, f32[1024,4096]{1,0:T(8,128)}) fusion(f32[4096]{0:T(1024)S(1)} %copy-done.117, bf16[1024,4096]{1,0:T(8,128)(2,1)} %all-gather.33.cloned.1.call-done, bf16[1,1024,1024]{2,1,0:T(8,128)(2,1)} %all-gather.31.cloned.1.call-done), kind=kOutput, calls=%fused_computation.115 | convolution fusion | flops 8866758656 | bytes 52445184 | tf_op jit(solution)/shard_map/srk,kn->srn/dot_general | solution.py:31
  566.0 82.2 %all-gather.35.cloned.1.call-done = bf16[4096,1024]{0,1:T(8,128)(2,1)} async-done(((bf16[4096,64]{0,1:T(8,128)(2,1)}), bf16[4096,1024]{0,1:T(8,128)(2,1)}) %all-gather.35.cloned.1.call-update) | async-done | bytes 8388624 | tf_op jit(solution)/shard_map/all_gather | solution.py:201
  648.2 26.6 %convert_reduce_fusion = (f32[4096]{0:T(1024)}, bf16[1024,4096]{1,0:T(8,128)(2,1)}) fusion(f32[1024,4096]{1,0:T(8,128)} %get-tuple-element.682, bf16[4096,1024]{0,1:T(8,128)(2,1)} %all-gather.35.cloned.1.call-done, bf16[1,1024,1024]{2,1,0:T(8,128)(2,1)} %all-gather.37.cloned.1.call-done, f32[1024,4096]{1,0:T(8,128)} %get-tuple-element.709, ...), kind=kOutput, calls=%fused_computation.113 | convolution fusion | flops 8661233664 | bytes 52461568 | tf_op jit(solution)/shard_map/srn,kn->srk/dot_general | solution.py:35
  674.7 14.9 convert_bitcast_fusion.1
  689.8 15.2 convert_bitcast_fusion.2
  736.5 50.7 %while.62 = (s32[]{:T(128)}, f32[1,512,8,64]{1,3,2,0:T(8,128)S(1)}, f32[1,512,8,64]{1,3,2,0:T(8,128)}, bf16[2,512,8,64]{1,3,2,0:T(8,128)(2,1)}, s32[2]{0:T(128)S...) while((s32[]{:T(128)}, f32[1,512,8,64]{1,3,2,0:T(8,128)S(1)}, ...), condition=%wide.region_22.23_spmd, body=%wide.region_20.22_spmd.sunk | while | flops 1374941184 | bytes 110748152 | solution.py:156
  836.6 116.6 %while.63 = (s32[]{:T(128)}, f32[1,1024,8,64]{1,3,2,0:T(8,128)}, f32[1,1024,8,64]{1,3,2,0:T(8,128)}, bf16[2,512,8,64]{1,3,2,0:T(8,128)(2,1)}, s32[2]{0:T(128)S(1...) while((s32[]{:T(128)}, f32[1,1024,8,64]{1,3,2,0:T(8,128)}, ...), condition=%wide.region_28.29_spmd, body=%wide.region_26.28_spmd.sunk | while | flops 2725507584 | bytes 305232480 | solution.py:156
  853.0 16.5 multiply_reduce_fusion.7
  911.0 16.3 multiply_reduce_fusion.7
  1014.0 14.7 fusion.123
  1033.1 77.4 %all-reduce.2 = (f32[4,512]{1,0:T(4,128)}, f32[4096]{0:T(1024)}) all-reduce(f32[4,512]{1,0:T(4,128)S(1)} %pad_maximum_fusion.3, f32[4096]{0:T(1024)S(1)} %copy-done.105), channel_id=1, replica_groups=mesh['dp'=16,'mp'=2] {'dp'}, use_global_device_ids=true, to_apply=%region_48.49 | all-reduce | flops 6144 | bytes 49152 | tf_op jit(solution)/shard_map/psum | solution.py:314
  1115.2 38.8 %all-reduce.1 = (f32[3,1024]{1,0:T(4,128)}, f32[6,1024]{1,0:T(8,128)}) all-reduce(f32[3,1024]{1,0:T(4,128)S(1)} %pad_maximum_fusion.2, f32[6,1024]{1,0:T(8,128)S(1)} %stack.79), channel_id=1, replica_groups=mesh['dp'=16,'mp'=2] {'dp','mp'}, use_global_device_ids=true, to_apply=%region_36.37 | all-reduce | flops 9216 | bytes 73728 | tf_op jit(solution)/shard_map/psum | solution.py:310
  1157.0 33.6 %reduce-scatter.34.cloned.1.call-done = f32[512,64]{0,1:T(8,128)} async-done(((f32[512,1024]{0,1:T(8,128)}), f32[512,64]{0,1:T(8,128)}) %reduce-scatter.34.cloned.1.call-update) | async-done | bytes 131088 | tf_op jit(solution)/shard_map/reduce_scatter | solution.py:302
  1190.6 80.6 %reduce-scatter.30.cloned.1.call-done = f32[512,64]{0,1:T(8,128)} async-done(((f32[512,1024]{0,1:T(8,128)}), f32[512,64]{0,1:T(8,128)}) %reduce-scatter.30.cloned.1.call-update) | async-done | bytes 131088 | tf_op jit(solution)/shard_map/reduce_scatter | solution.py:299
  1271.2 136.1 %reduce-scatter.28.cloned.1.call-done = f32[3,64,512]{2,1,0:T(8,128)} async-done(((f32[3,1024,512]{2,1,0:T(8,128)}), f32[3,64,512]{2,1,0:T(8,128)}) %reduce-scatter.28.cloned.1.call-update) | async-done | bytes 393232 | tf_op jit(solution)/shard_map/reduce_scatter | solution.py:298
  1407.2 350.5 %reduce-scatter.36.cloned.1.call-done = f32[64,4096]{1,0:T(8,128)} async-done(((f32[1024,4096]{1,0:T(8,128)}), f32[64,4096]{1,0:T(8,128)}) %reduce-scatter.36.cloned.1.call-update) | async-done | bytes 1048592 | tf_op jit(solution)/shard_map/reduce_scatter | solution.py:303
  1757.7 354.9 %reduce-scatter.38.cloned.1.call-done = f32[4096,64]{0,1:T(8,128)} async-done(((f32[4096,1024]{0,1:T(8,128)}), f32[4096,64]{0,1:T(8,128)}) %reduce-scatter.38.cloned.1.call-update) | async-done | bytes 1048592 | tf_op jit(solution)/shard_map/reduce_scatter | solution.py:304
  (532 shorter events, 438.8 us)
Async XLA Ops:
  14.3 85.6 %all-gather.17.cloned.1.call-start = ((), (), s32[]{:S(2)}) async-start(), calls=%async_computation.14 | async-start | bytes 3342336 | tf_op jit(solution)/shard_map/all_gather | solution.py:195
  15.1 142.6 %all-gather.19.cloned.1.call-start = ((), (), s32[]{:S(2)}) async-start(), calls=%async_computation.15 | async-start | bytes 1114112 | tf_op jit(solution)/shard_map/all_gather | solution.py:196
  15.8 154.3 %reduce-scatter.14.cloned.1.call-start = ((), (), s32[]{:S(2)}) async-start(), calls=%async_computation.16 | async-start | bytes 3145728 | tf_op jit(solution)/shard_map/reduce_scatter | solution.py:65
  162.2 85.1 %all-gather.27.cloned.1.call-start = ((), (), s32[]{:S(2)}) async-start(), calls=%async_computation.20 | async-start | bytes 2228224 | tf_op jit(solution)/shard_map/all_gather | solution.py:198
  163.2 141.7 %all-gather.23.cloned.1.call-start = ((), (), s32[]{:S(2)}) async-start(), calls=%async_computation.18 | async-start | bytes 1114112 | tf_op jit(solution)/shard_map/all_gather | solution.py:197
  163.9 152.6 %all-gather.21.cloned.1.call-start = ((), (), s32[]{:S(2)}) async-start(), calls=%async_computation.17 | async-start | bytes 3145728 | tf_op jit(solution)/shard_map/all_gather | solution.py:57
  174.2 202.5 %all-gather.29.cloned.1.call-start = ((), (), s32[]{:S(2)}) async-start(), calls=%async_computation.21 | async-start | bytes 1114112 | tf_op jit(solution)/shard_map/all_gather | solution.py:199
  174.9 214.5 %reduce-scatter.16.cloned.1.call-start = ((), (), s32[]{:S(2)}) async-start(), calls=%async_computation.22 | async-start | bytes 3145728 | tf_op jit(solution)/shard_map/reduce_scatter | solution.py:65
  380.9 126.0 %all-gather.33.cloned.1.call-start = ((), (), s32[]{:S(2)}) async-start(), calls=%async_computation.24 | async-start | bytes 8912896 | tf_op jit(solution)/shard_map/all_gather | solution.py:200
  382.9 134.7 %all-gather.31.cloned.1.call-start = ((), (), s32[]{:S(2)}) async-start(), calls=%async_computation.23 | async-start | bytes 3145728 | tf_op jit(solution)/shard_map/all_gather | solution.py:57
  394.0 171.9 %all-gather.37.cloned.1.call-start = ((), (), s32[]{:S(2)}) async-start(), calls=%async_computation.27 | async-start | bytes 3145728 | tf_op jit(solution)/shard_map/all_gather | solution.py:57
  394.8 253.4 %all-gather.35.cloned.1.call-start = ((), (), s32[]{:S(2)}) async-start(), calls=%async_computation.25 | async-start | bytes 8912896 | tf_op jit(solution)/shard_map/all_gather | solution.py:201
  395.7 309.3 %reduce-scatter.20.cloned.1.call-start = ((), (), s32[]{:S(2)}) async-start(), calls=%async_computation.28 | async-start | bytes 3145728 | tf_op jit(solution)/shard_map/reduce_scatter | solution.py:65
  718.3 86.0 %reduce-scatter.22.cloned.1.call-start = ((), (), s32[]{:S(2)}) async-start(), calls=%async_computation.30 | async-start | bytes 3145728 | tf_op jit(solution)/shard_map/reduce_scatter | solution.py:65
  793.4 34.0 %all-gather.41.cloned.1.call-start = ((), (), s32[]{:S(2)}) async-start(), calls=%async_computation.31 | async-start | bytes 3145728 | tf_op jit(solution)/shard_map/all_gather | solution.py:57
  813.8 217.2 %all-reduce.5.cloned.1.call-start = ((), (), s32[]{:S(2)}) async-start(), calls=%async_computation.40 | async-start | bytes 8388608
  827.4 283.2 %reduce-scatter.24.cloned.1.call-start = ((), (), s32[]{:S(2)}) async-start(), calls=%async_computation.32 | async-start | bytes 3145728 | tf_op jit(solution)/shard_map/reduce_scatter | solution.py:65
  965.4 191.6 %reduce-scatter.26.cloned.1.call-start = ((), (), s32[]{:S(2)}) async-start(), calls=%async_computation.33 | async-start | bytes 1572864 | tf_op jit(solution)/shard_map/reduce_scatter | solution.py:65
  970.5 186.5 %reduce-scatter.32.cloned.1.call-start = ((), (), s32[]{:S(2)}) async-start(), calls=%async_computation.36 | async-start | bytes 2228224 | tf_op jit(solution)/shard_map/reduce_scatter | solution.py:300
  975.1 215.5 %reduce-scatter.34.cloned.1.call-start = ((), (), s32[]{:S(2)}) async-start(), calls=%async_computation.37 | async-start | bytes 2228224 | tf_op jit(solution)/shard_map/reduce_scatter | solution.py:302
  980.5 290.6 %reduce-scatter.30.cloned.1.call-start = ((), (), s32[]{:S(2)}) async-start(), calls=%async_computation.35 | async-start | bytes 2228224 | tf_op jit(solution)/shard_map/reduce_scatter | solution.py:299
  986.0 421.3 %reduce-scatter.28.cloned.1.call-start = ((), (), s32[]{:S(2)}) async-start(), calls=%async_computation.34 | async-start | bytes 6684672 | tf_op jit(solution)/shard_map/reduce_scatter | solution.py:298
  996.2 761.5 %reduce-scatter.36.cloned.1.call-start = ((), (), s32[]{:S(2)}) async-start(), calls=%async_computation.38 | async-start | bytes 17825792 | tf_op jit(solution)/shard_map/reduce_scatter | solution.py:303
  1012.4 1100.1 %reduce-scatter.38.cloned.1.call-start = ((), (), s32[]{:S(2)}) async-start(), calls=%async_computation.39 | async-start | bytes 17825792 | tf_op jit(solution)/shard_map/reduce_scatter | solution.py:304
  (143 other events, 1922.8 us)
Sparse Core Ops, SparseCore 0:
  14.4 13.2 all-gather.14
  31.1 68.7 all-gather.16
  103.2 54.4 all-gather.18
  171.6 10.2 all-gather.24
  185.4 61.8 all-gather.26
  251.0 53.8 all-gather.22
  307.1 9.3 all-gather.20
  320.2 56.4 all-gather.28
  392.8 114.0 all-gather.32
  508.8 8.7 all-gather.30
  519.1 11.7 all-gather.36
  534.1 113.9 all-gather.34
  718.4 11.7 all-gather.38
  793.5 10.7 reduce-scatter.21
  813.9 11.7 all-gather.40
  832.1 169.3 all-reduce.4
  1003.8 8.5 reduce-scatter.23
  1015.2 9.7 reduce-scatter.25
  1027.9 82.1 reduce-scatter.31
  1112.7 77.7 reduce-scatter.33
  1193.4 77.6 reduce-scatter.29
  1273.9 133.3 reduce-scatter.27
  1410.0 347.6 reduce-scatter.35
  1760.6 351.9 reduce-scatter.37
  (4 shorter events, 31.7 us)
where the time goes:
time: 2130 us; the launch traced here: 2120 us
  waiting for transfers between devices  1470 us (69%)
  matrix products  348 us (16%)
  blocking collectives  116 us (5%)
  other arithmetic  87.7 us (4%)
  local copies, waits for them, and re-layouts  58.3 us (3%)
  loops' own time  22.2 us (1%)
    reduce_scatter x1, waiting for transfers between devices, per_device(): lax.psum_scatter(d_down_weight, 'dp', scatter_dimension=1, tiled=True)  355 us
    reduce_scatter x1, waiting for transfers between devices, per_device(): lax.psum_scatter(d_up_weight, 'dp', scatter_dimension=0, tiled=True)  350 us
    reduce_scatter x1, waiting for transfers between devices, per_device(): lax.psum_scatter(d_self_proj, 'dp', scatter_dimension=1, tiled=True)  136 us
    all_gather x1, waiting for transfers between devices, per_device(): lax.all_gather(up_weight.astype(jnp.bfloat16), 'dp', axis=0, tiled=True)  111 us
    dot_general x10, matrix products, project(): jnp.einsum('srk,kn->srn', operand, weight, preferred_element_type=jnp.flo...  84.7 us
    all_gather x1, waiting for transfers between devices, per_device(): lax.all_gather(down_weight.astype(jnp.bfloat16), 'dp', axis=1, tiled=True)  82.2 us
    reduce_scatter x1, waiting for transfers between devices, per_device(): lax.psum_scatter(d_self_out, 'dp', scatter_dimension=1, tiled=True)  80.6 us
    psum x1, blocking collectives, per_device(): d_head_biases, d_up_bias = lax.psum((head_rows, d_up_bias), 'dp')  77.4 us
  transfers between devices with their start and end apart: 28, of which 21 were waited for; matrix products, arithmetic and copies ran while one was open for 17% of the time, Pallas kernels for 0%

commit v1 on v0

v1 whole, which is shorter than its diff:
```python
import functools
import math

import jax
import jax.numpy as jnp
from jax import lax
from jax.experimental import pallas as pl
from jax.experimental.pallas import tpu as pltpu
from jax.sharding import Mesh
from jax.sharding import PartitionSpec as P

HEAD = 64
PAIR = 2 * HEAD
F32 = jnp.float32
BF16 = jnp.bfloat16
VMEM_LIMIT = 56 * 1024 * 1024
MASKED = -1e30


def dot(left, right, left_dim, right_dim):
    return lax.dot_general(
        left, right, (((left_dim,), (right_dim,)), ((), ())), preferred_element_type=F32
    )


def normalize(values, gain_row, shift_row):
    average = jnp.mean(values, axis=-1, keepdims=True)
    centred = values - average
    spread = jnp.mean(centred * centred, axis=-1, keepdims=True)
    return centred * lax.rsqrt(spread + 1e-05) * gain_row + shift_row


def row_total(rows):
    return jnp.sum(rows.astype(F32), axis=0)


def swap(values, axis):
    return lax.ppermute(values, axis, [(0, 1), (1, 0)])


def in_order(own, other, index, dim):
    first = jnp.where(index == 0, own, other)
    second = jnp.where(index == 0, other, own)
    return first, second


def both(own, axis, dim):
    return jnp.concatenate(in_order(own, swap(own, axis), lax.axis_index(axis), dim), dim)


def gather_line(block, axis, size):
    if size > 4:
        return lax.all_gather(block, axis, axis=0, tiled=False)
    me = lax.axis_index(axis)
    whole = jnp.zeros((size,) + block.shape, block.dtype)
    whole = lax.dynamic_update_index_in_dim(whole, block, me, 0)
    for step in range(1, size):
        got = lax.ppermute(block, axis, [(at, (at + step) % size) for at in range(size)])
        whole = lax.dynamic_update_index_in_dim(whole, got, lax.rem(me - step + size, size), 0)
    return whole


def scatter_line(blocks, axis, size):
    if size > 4:
        return lax.psum_scatter(blocks.astype(F32), axis, scatter_dimension=0, tiled=False)
    me = lax.axis_index(axis)
    total = lax.dynamic_index_in_dim(blocks, me, 0, False).astype(F32)
    for step in range(1, size):
        block = lax.dynamic_index_in_dim(blocks, lax.rem(me + step, size), 0, False)
        got = lax.ppermute(block, axis, [(at, (at + step) % size) for at in range(size)])
        total = total + got.astype(F32)
    return total


def gather_pair(blocks, axis, dim):
    own, other = blocks, swap(blocks, axis)
    return jnp.stack(in_order(own, other, lax.axis_index(axis), dim), dim)


def scatter_pair(blocks, axis, dim):
    me = lax.axis_index(axis)
    keep = lax.dynamic_index_in_dim(blocks, me, dim, False)
    send = lax.dynamic_index_in_dim(blocks, 1 - me, dim, False)
    return (keep.astype(F32) + swap(send, axis).astype(F32)).astype(BF16)


def halves(values, low):
    zero = jnp.zeros_like(values)
    return jnp.where(low, values, zero), jnp.where(low, zero, values)


def low_lanes():
    return lax.broadcasted_iota(jnp.int32, (1, PAIR), 1) < HEAD


def forward_kernel(causal, tile, q_ref, k_ref, v_ref, row_ref, col_ref, o_ref, log_ref):
    length, width = q_ref.shape[0], k_ref.shape[0]
    low = low_lanes()
    for number in range(length // tile):
        rows = pl.ds(number * tile, tile)
        q_parts = halves(q_ref[rows, :] * 0.125, low)
        spans = [(0, width)]
        if causal:
            spans = [(0, number * tile)] if number else []
            spans.append((number * tile, tile))
        allowed = []
        for start, size in spans:
            same = row_ref[rows, :] == col_ref[:, pl.ds(start, size)]
            if causal and start == number * tile:
                same = same & (
                    lax.broadcasted_iota(jnp.int32, (tile, size), 0)
                    >= lax.broadcasted_iota(jnp.int32, (tile, size), 1)
                )
            allowed.append(same)
        result = jnp.zeros((tile, PAIR), F32)
        tops, sums = [], []
        for half in range(2):
            scores = []
            for (start, size), same in zip(spans, allowed):
                part = dot(q_parts[half], k_ref[pl.ds(start, size), :], 1, 1)
                scores.append(jnp.where(same, part, MASKED))
            top = functools.reduce(
                jnp.maximum, [jnp.max(part, axis=1, keepdims=True) for part in scores]
            )
            summed = jnp.zeros((tile, 1), F32)
            for (start, size), part in zip(spans, scores):
                chance = jnp.exp(part - top)
                summed = summed + jnp.sum(chance, axis=1, keepdims=True)
                v_part = halves(v_ref[pl.ds(start, size), :], low)[half]
                result = result + dot(chance.astype(BF16), v_part, 1, 0)
            tops.append(top)
            sums.append(summed)
        total = jnp.where(low, sums[0], sums[1])
        o_ref[rows, :] = (result / total).astype(BF16)
        logs = jnp.where(low, tops[0], tops[1]) + jnp.log(total)
        flipped = logs.T
        log_ref[0, 0:1, rows] = flipped[0:1, :]
        log_ref[0, 1:2, rows] = flipped[HEAD : HEAD + 1, :]


def backward_kernel(
    causal,
    tile,
    q_ref,
    k_ref,
    v_ref,
    o_ref,
    g_ref,
    log_ref,
    row_ref,
    col_ref,
    dq_ref,
    dk_ref,
    dv_ref,
    dk_sum,
    dv_sum,
):
    length, width = q_ref.shape[0], k_ref.shape[0]
    low = low_lanes()
    dk_sum[...] = jnp.zeros_like(dk_sum)
    dv_sum[...] = jnp.zeros_like(dv_sum)
    for number in range(length // tile):
        rows = pl.ds(number * tile, tile)
        q_parts = halves(q_ref[rows, :] * 0.125, low)
        grad = g_ref[rows, :]
        g_parts = halves(grad, low)
        product = (grad.astype(F32) * o_ref[rows, :].astype(F32)).T
        deltas = [
            jnp.sum(product[:HEAD], axis=0, keepdims=True),
            jnp.sum(product[HEAD:], axis=0, keepdims=True),
        ]
        dq = jnp.zeros((tile, PAIR), F32)
        for other in range(number + 1 if causal else width // tile):
            cols = pl.ds(other * tile, tile)
            same = col_ref[cols, :] == row_ref[:, rows]
            if causal and other == number:
                same = same & (
                    lax.broadcasted_iota(jnp.int32, (tile, tile), 1)
                    >= lax.broadcasted_iota(jnp.int32, (tile, tile), 0)
                )
            key, value = k_ref[cols, :], v_ref[cols, :]
            k_parts = halves(key, low)
            dk = jnp.zeros((tile, PAIR), F32)
            dv = jnp.zeros((tile, PAIR), F32)
            for half in range(2):
                scores = jnp.where(same, dot(key, q_parts[half], 1, 1), MASKED)
                chance = jnp.exp(scores - log_ref[0, half : half + 1, rows])
                dv = dv + dot(chance.astype(BF16), g_parts[half], 1, 0)
                change = dot(value, g_parts[half], 1, 1)
                inner = (chance * (change - deltas[half])).astype(BF16)
                dk = dk + dot(inner, q_parts[half], 1, 0)
                dq = dq + dot(inner, k_parts[half], 0, 0)
            dk_sum[cols, :] += dk
            dv_sum[cols, :] += dv
        dq_ref[rows, :] = (dq * 0.125).astype(BF16)
    dk_ref[...] = dk_sum[...].astype(BF16)
    dv_ref[...] = dv_sum[...].astype(BF16)


def attention_cost(length, width, features, products):
    return pl.CostEstimate(
        flops=8 * products * length * width * features,
        bytes_accessed=2 * features * (2 * length + 2 * width),
        transcendentals=length * width * features // HEAD,
    )


def attend(queries, keys, values, row_docs, col_docs, causal):
    length, features = queries.shape
    width = keys.shape[0]
    tile = min(256, length)
    at = lambda size: pl.BlockSpec((size, PAIR), lambda pair: (0, pair))
    fixed = lambda shape: pl.BlockSpec(shape, lambda pair: (0, 0))
    return pl.pallas_call(
        functools.partial(forward_kernel, causal, tile),
        grid=(features // PAIR,),
        in_specs=[at(length), at(width), at(width), fixed((length, 1)), fixed((1, width))],
        out_specs=[at(length), pl.BlockSpec((1, 2, length), lambda pair: (pair, 0, 0))],
        out_shape=[
            jax.ShapeDtypeStruct((length, features), BF16),
            jax.ShapeDtypeStruct((features // PAIR, 2, length), F32),
        ],
        compiler_params=pltpu.CompilerParams(vmem_limit_bytes=VMEM_LIMIT),
        cost_estimate=attention_cost(length, width, features, 2),
    )(queries, keys, values, row_docs[:, None], col_docs[None, :])


def attend_back(queries, keys, values, result, grad, logs, row_docs, col_docs, causal):
    length, features = queries.shape
    width = keys.shape[0]
    tile = min(256, length, width)
    at = lambda size: pl.BlockSpec((size, PAIR), lambda pair: (0, pair))
    fixed = lambda shape: pl.BlockSpec(shape, lambda pair: (0, 0))
    return pl.pallas_call(
        functools.partial(backward_kernel, causal, tile),
        grid=(features // PAIR,),
        in_specs=[
            at(length),
            at(width),
            at(width),
            at(length),
            at(length),
            pl.BlockSpec((1, 2, length), lambda pair: (pair, 0, 0)),
            fixed((1, length)),
            fixed((width, 1)),
        ],
        out_specs=[at(length), at(width), at(width)],
        out_shape=[
            jax.ShapeDtypeStruct((length, features), BF16),
            jax.ShapeDtypeStruct((width, features), BF16),
            jax.ShapeDtypeStruct((width, features), BF16),
        ],
        scratch_shapes=[pltpu.VMEM((width, PAIR), F32), pltpu.VMEM((width, PAIR), F32)],
        compiler_params=pltpu.CompilerParams(vmem_limit_bytes=VMEM_LIMIT),
        cost_estimate=attention_cost(length, width, features, 5),
    )(queries, keys, values, result, grad, logs, row_docs[None, :], col_docs[:, None])


def gelu_and_slope(values):
    tail = jnp.exp(values * values * -0.5)
    step = 1.0 / (1.0 + (0.3275911 * math.sqrt(0.5)) * jnp.abs(values))
    series = 1.061405429
    for factor in (-1.453152027, 1.421413741, -0.284496736, 0.254829592):
        series = series * step + factor
    outside = (0.5 * series) * step * tail
    below = jnp.where(values >= 0, 1.0 - outside, outside)
    return values * below, below + values * tail * (1.0 / math.sqrt(2.0 * math.pi))


def hidden_kernel(piece, x_ref, g_ref, up_ref, down_ref, bias_ref, act_ref, grad_ref):
    for number in range(x_ref.shape[0] // piece):
        rows = pl.ds(number * piece, piece)
        before = dot(x_ref[rows, :], up_ref[...], 1, 0) + bias_ref[...]
        act, slope = gelu_and_slope(before)
        act_ref[rows, :] = act.astype(BF16)
        raw = dot(g_ref[rows, :], down_ref[...], 1, 0)
        grad_ref[rows, :] = (raw * slope).astype(BF16)


def hidden_parts(normed, grad, up, down_rows, bias_row):
    rows, features = normed.shape
    hidden = up.shape[1]
    tile = min(512, hidden)
    whole = pl.BlockSpec((rows, features), lambda step: (0, 0))
    piece = lambda height: pl.BlockSpec((height, tile), lambda step: (0, step))
    return pl.pallas_call(
        functools.partial(hidden_kernel, min(256, rows)),
        grid=(hidden // tile,),
        in_specs=[whole, whole, piece(features), piece(features), piece(1)],
        out_specs=[piece(rows), piece(rows)],
        out_shape=[jax.ShapeDtypeStruct((rows, hidden), BF16)] * 2,
        compiler_params=pltpu.CompilerParams(vmem_limit_bytes=VMEM_LIMIT),
        cost_estimate=pl.CostEstimate(
            flops=4 * rows * features * hidden,
            bytes_accessed=4 * (rows * features + features * hidden + rows * hidden),
            transcendentals=rows * hidden,
        ),
    )(normed, grad, up, down_rows, bias_row)


def per_device(
    line,
    tokens,
    memory,
    segments,
    sources,
    gains,
    biases,
    head_biases,
    self_proj,
    self_out,
    cross_query,
    cross_kv,
    cross_out,
    up_weight,
    up_bias,
    down_weight,
    cotangent,
):
    at_x, at_core = lax.axis_index("x"), lax.axis_index("core")
    row_docs, col_docs = segments[0], sources[0]
    half_rows, features = tokens.shape[1:]
    heads_width = self_out.shape[0]
    part_rows = self_out.shape[1]
    hidden_part = up_weight.shape[1] // 2

    def gather_attention(shard):
        blocks = gather_line(shard, "z", line)
        blocks = gather_pair(blocks, "y", 1)
        blocks = gather_pair(blocks, "x", 2)
        return blocks.reshape(features, shard.shape[1])

    def gather_hidden(shard):
        keep = lax.dynamic_slice_in_dim(shard, at_x * hidden_part, hidden_part, 1)
        send = lax.dynamic_slice_in_dim(shard, (1 - at_x) * hidden_part, hidden_part, 1)
        rows = jnp.concatenate(in_order(keep, swap(send, "x"), at_x, 0), 0)
        blocks = gather_pair(gather_line(rows, "z", line), "y", 1)
        return blocks.reshape(features, hidden_part)

    def scatter_attention(grad):
        blocks = grad.reshape(line, 2, 2, part_rows, grad.shape[1])
        blocks = scatter_pair(blocks, "x", 2)
        blocks = scatter_pair(blocks, "y", 1)
        return scatter_line(blocks, "z", line)

    def scatter_hidden(grad):
        blocks = scatter_pair(grad.reshape(line, 2, 2 * part_rows, hidden_part), "y", 1)
        rows = scatter_line(blocks, "z", line).reshape(2, part_rows, hidden_part)
        keep = lax.dynamic_index_in_dim(rows, at_x, 0, False)
        send = lax.dynamic_index_in_dim(rows, 1 - at_x, 0, False).astype(BF16)
        return jnp.concatenate(in_order(keep, swap(send, "x").astype(F32), at_x, 1), 1)

    def own_rows(values):
        return lax.dynamic_slice_in_dim(values, at_core * half_rows, half_rows, 0)

    def summed(partial):
        short = partial.astype(BF16)
        return short.astype(F32) + swap(short, "core").astype(F32)

    def summed_rows(partial):
        short = partial.astype(BF16)
        pieces = short.reshape(2, short.shape[0] // 2, short.shape[1])
        keep = lax.dynamic_index_in_dim(pieces, at_core, 0, False)
        send = lax.dynamic_index_in_dim(pieces, 1 - at_core, 0, False)
        return keep.astype(F32) + swap(send, "core").astype(F32)

    def short(part):
        return part.astype(BF16)

    first = gather_attention(
        jnp.concatenate([short(self_proj[0]), short(self_proj[1]), short(self_proj[2])], 1)
    )
    second = gather_attention(
        jnp.concatenate(
            [
                short(self_out).T,
                short(cross_query),
                short(cross_kv[0]),
                short(cross_kv[1]),
                short(cross_out).T,
            ],
            1,
        )
    )
    up = gather_hidden(short(up_weight))
    down_rows = gather_hidden(short(down_weight).T)
    column = lambda whole, number: whole[:, number * heads_width : (number + 1) * heads_width]
    w_query, w_key, w_value = (column(first, number) for number in range(3))
    w_out, w_cross_query, w_cross_key, w_cross_value, w_cross_out = (
        column(second, number) for number in range(5)
    )
    bias_part = lax.dynamic_slice_in_dim(up_bias, at_x * hidden_part, hidden_part, 0)[None, :]

    rows_in = both(tokens[0], "core", 0).astype(F32)
    mem_rows = both(memory[0], "core", 0)
    grad_mine = cotangent[0]
    grad_theirs = swap(grad_mine, "x")
    grad_own = both(grad_mine, "core", 0)
    grad_other = both(grad_theirs, "core", 0)

    norm_one, back_one = jax.vjp(normalize, rows_in, gains[0], biases[0])
    norm_one = short(norm_one)
    queries = short(dot(norm_one, w_query, 1, 0) + head_biases[0])
    keys = short(dot(norm_one, w_key, 1, 0))
    values = short(dot(norm_one, w_value, 1, 0) + head_biases[1])
    attended, logs_self = attend(queries, keys, values, row_docs, row_docs, True)
    after_self = rows_in + summed(dot(attended, w_out, 1, 1)) + biases[1]
    norm_two, back_two = jax.vjp(normalize, after_self, gains[1], biases[2])
    norm_two = short(norm_two)
    cross_queries = short(dot(norm_two, w_cross_query, 1, 0) + head_biases[2])
    cross_keys = short(dot(mem_rows, w_cross_key, 1, 0))
    cross_values = short(dot(mem_rows, w_cross_value, 1, 0) + head_biases[3])
    cross_attended, logs_cross = attend(
        cross_queries, cross_keys, cross_values, row_docs, col_docs, False
    )
    after_cross = after_self + summed(dot(cross_attended, w_cross_out, 1, 1)) + biases[3]
    after_cross_mine = own_rows(after_cross)
    norm_three, back_three = jax.vjp(normalize, after_cross_mine, gains[2], biases[4])
    norm_three = short(norm_three)

    norm_own = both(norm_three, "core", 0)
    norm_other = both(swap(norm_three, "x"), "core", 0)
    act_own, hid_own = hidden_parts(norm_own, grad_own, up, down_rows, bias_part)
    act_other, hid_other = hidden_parts(norm_other, grad_other, up, down_rows, bias_part)

    def over_pair(own, other):
        own_part, other_part = summed_rows(own), summed_rows(other)
        return own_part + swap(short(other_part), "x").astype(F32)

    d_norm_three = over_pair(dot(hid_own, up, 1, 1), dot(hid_other, up, 1, 1))
    d_down = short(dot(grad_own, act_own, 0, 0) + dot(grad_other, act_other, 0, 0))
    d_up = short(dot(norm_own, hid_own, 0, 0) + dot(norm_other, hid_other, 0, 0))
    d_down_weight = scatter_hidden(d_down).T
    d_up_weight = scatter_hidden(d_up)
    fed = over_pair(dot(act_own, down_rows, 1, 1), dot(act_other, down_rows, 1, 1))
    layer_out = short(after_cross_mine + fed + biases[5])
    d_up_bias = row_total(hid_own) + row_total(hid_other)

    grad_rows = grad_mine.astype(F32)
    d_bias_five = row_total(grad_rows)
    back_rows, d_gain_two, d_bias_four = back_three(d_norm_three)
    d_cross_res = grad_rows + back_rows
    d_bias_three = row_total(d_cross_res)
    res_rows = both(short(d_cross_res), "core", 0)
    d_cross_out = dot(res_rows, cross_attended, 0, 0)
    d_cross_att = short(dot(res_rows, w_cross_out, 1, 0))
    cq_grad, ck_grad, cv_grad = attend_back(
        cross_queries,
        cross_keys,
        cross_values,
        cross_attended,
        d_cross_att,
        logs_cross,
        row_docs,
        col_docs,
        False,
    )
    d_norm_two = summed(dot(cq_grad, w_cross_query, 1, 1))
    d_memory = short(
        summed_rows(dot(ck_grad, w_cross_key, 1, 1) + dot(cv_grad, w_cross_value, 1, 1))
    )
    d_cross_weights = scatter_attention(
        jnp.concatenate(
            [
                short(d_cross_out),
                short(dot(norm_two, cq_grad, 0, 0)),
                short(dot(mem_rows, ck_grad, 0, 0)),
                short(dot(mem_rows, cv_grad, 0, 0)),
            ],
            1,
        )
    )
    back_rows, d_gain_one, d_bias_two = back_two(d_norm_two)
    d_self_res = res_rows.astype(F32) + back_rows
    d_bias_one = row_total(d_self_res)
    self_rows = short(d_self_res)
    d_self_out = short(dot(self_rows, attended, 0, 0))
    d_attended = short(dot(self_rows, w_out, 1, 0))
    q_grad, k_grad, v_grad = attend_back(
        queries, keys, values, attended, d_attended, logs_self, row_docs, row_docs, True
    )
    d_self_weights = scatter_attention(
        jnp.concatenate(
            [
                d_self_out,
                short(dot(norm_one, q_grad, 0, 0)),
                short(dot(norm_one, k_grad, 0, 0)),
                short(dot(norm_one, v_grad, 0, 0)),
            ],
            1,
        )
    )
    d_norm_one = summed(
        dot(q_grad, w_query, 1, 1) + dot(k_grad, w_key, 1, 1) + dot(v_grad, w_value, 1, 1)
    )
    back_rows, d_gain_zero, d_bias_zero = back_one(d_norm_one)
    d_tokens = short(own_rows(d_self_res + back_rows))

    small = jnp.stack(
        [
            d_gain_zero * 0.5,
            d_gain_one * 0.5,
            d_gain_two,
            d_bias_zero * 0.5,
            d_bias_one * 0.5,
            d_bias_two * 0.5,
            d_bias_three,
            d_bias_four,
            d_bias_five,
        ]
    )
    head_rows = jnp.stack(
        [row_total(q_grad), row_total(v_grad), row_total(cq_grad), row_total(cv_grad)]
    )
    head_place = jnp.zeros((4, 2, heads_width), F32)
    head_place = lax.dynamic_update_slice(head_place, head_rows[:, None], (0, at_core, 0))
    bias_place = jnp.zeros((2, 2, hidden_part), F32)
    bias_place = lax.dynamic_update_slice(
        bias_place, d_up_bias[None, None], (at_core, at_x, 0)
    )
    totals = lax.psum(
        jnp.concatenate([small.reshape(-1), head_place.reshape(-1), bias_place.reshape(-1)]),
        ("z", "y", "x", "core"),
    )
    count, head_count = small.size, head_place.size
    small = totals[:count].reshape(small.shape)
    head_place = totals[count : count + head_count].reshape(head_place.shape)
    bias_place = totals[count + head_count :].reshape(2, 2 * hidden_part)
    d_head_biases = lax.dynamic_index_in_dim(head_place, at_core, 1, False)
    d_up_bias = lax.dynamic_index_in_dim(bias_place, at_core, 0, False)

    return (
        layer_out[None],
        d_tokens[None],
        d_memory[None],
        small[:3],
        small[3:],
        d_head_biases,
        jnp.stack([column(d_self_weights, number) for number in (1, 2, 3)]),
        column(d_self_weights, 0).T,
        column(d_cross_weights, 1),
        jnp.stack([column(d_cross_weights, number) for number in (2, 3)]),
        column(d_cross_weights, 0).T,
        d_up_weight,
        d_up_bias,
        d_down_weight,
    )


def solution(mesh):
    members, cores = mesh.devices.shape
    line = members // 4
    parts = Mesh(mesh.devices.reshape(line, 2, 2, cores), ("z", "y", "x", "core"))
    dp = ("z", "y", "x")
    in_specs = (
        P(dp, "core", None),
        P(dp, "core", None),
        P(dp, None),
        P(dp, None),
        P(),
        P(),
        P(None, "core"),
        P(None, dp, "core"),
        P("core", dp),
        P(dp, "core"),
        P(None, dp, "core"),
        P("core", dp),
        P(dp, "core"),
        P("core"),
        P("core", dp),
        P(dp, "core", None),
    )
    out_specs = (
        P(dp, "core", None),
        P(dp, "core", None),
        P(dp, "core", None),
        P(),
        P(),
        P(None, "core"),
        P(None, dp, "core"),
        P("core", dp),
        P(dp, "core"),
        P(None, dp, "core"),
        P("core", dp),
        P(dp, "core"),
        P("core"),
        P("core", dp),
    )
    return jax.shard_map(
        functools.partial(per_device, line),
        mesh=parts,
        in_specs=in_specs,
        out_specs=out_specs,
        check_vma=False,
    )
```

time: 2130 us -> 946 us (0.44)
  waiting for transfers between devices: 1470 us -> 475 us
  matrix products: 348 us -> 97.4 us
  blocking collectives: 116 us -> 0 us
  Pallas kernels: 0 us -> 114 us
  starting transfers between devices: 2.76 us -> 60.7 us
  loops' own time: 22.2 us -> 0 us
    reduce_scatter x13 -> x0, waiting for transfers between devices: 982 us -> none  [the longest x1 355 us: per_device(): lax.psum_scatter(d_down_weight, 'dp', scatter_dimension=1, tiled=True)]
    all_gather x14 -> x0, waiting for transfers between devices: 485 us -> none  [the longest x1 111 us: per_device(): lax.all_gather(up_weight.astype(jnp.bfloat16), 'dp', axis=0, tiled=True)]
    ppermute x0 -> x60, waiting for transfers between devices: none -> 359 us  [the longest x36 255 us: swap(): return lax.ppermute(values, axis, [(0, 1), (1, 0)])]
    dot_general x58 -> x32, matrix products: 348 us -> 97.4 us  [dot(): lax.dot_general(left, right, (((left_dim,), (right_dim,)), ((), ())), pre...]
    psum x2 -> x0, blocking collectives: 116 us -> none  [the longest x1 77.4 us: per_device(): d_head_biases, d_up_bias = lax.psum((head_rows, d_up_bias), 'dp')]
    psum x0 -> x1, waiting for transfers between devices: none -> 115 us  [per_device(): lax.psum(jnp.concatenate([small.reshape(-1), head_place.reshape(-1), bias...]
    pallas_call x0 -> x6, Pallas kernels: none -> 114 us  [the longest x2 49.8 us: attend_back(): pl.pallas_call(functools.partial(backward_kernel, causal, tile), grid=(fe...]
    ppermute x0 -> x60, starting transfers between devices: none -> 60.7 us  [the longest x36 27.4 us: swap(): return lax.ppermute(values, axis, [(0, 1), (1, 0)])]
  transfers between devices with their start and end apart: 28 -> 61, of which waited for: 21 -> 23; matrix products, arithmetic and copies ran while one was open for 17% -> 26% of each run, Pallas kernels for 0% -> 10%
where the time goes in v1:
time: 946 us; the launch traced here: 935 us
  waiting for transfers between devices  475 us (50%)
  Pallas kernels  114 us (12%)
  other arithmetic  103 us (11%)
  matrix products  97.4 us (10%)
  local copies, waits for them, and re-layouts  69.7 us (7%)
  starting transfers between devices  60.7 us (6%)
  between operations  16.1 us (2%)
    ppermute x36, waiting for transfers between devices, swap(): return lax.ppermute(values, axis, [(0, 1), (1, 0)])  255 us
    psum x1, waiting for transfers between devices, per_device(): lax.psum(jnp.concatenate([small.reshape(-1), head_place.reshape(-1), bias...  115 us
    dot_general x32, matrix products, dot(): lax.dot_general(left, right, (((left_dim,), (right_dim,)), ((), ())), pre...  97.4 us
    ppermute x12, waiting for transfers between devices, scatter_line(): lax.ppermute(block, axis, [(at, (at + step) % size) for at in range(size)])  93.3 us
    pallas_call x2, Pallas kernels, attend_back(): pl.pallas_call(functools.partial(backward_kernel, causal, tile), grid=(fe...  49.8 us
    pallas_call x2, Pallas kernels, hidden_parts(): pl.pallas_call(functools.partial(hidden_kernel, min(256, rows)), grid=(hi...  37 us
    pallas_call x2, Pallas kernels, attend(): pl.pallas_call(functools.partial(forward_kernel, causal, tile), grid=(fea...  27.6 us
    ppermute x36, starting transfers between devices, swap(): return lax.ppermute(values, axis, [(0, 1), (1, 0)])  27.4 us
  transfers between devices with their start and end apart: 61, of which 23 were waited for; matrix products, arithmetic and copies ran while one was open for 26% of the time, Pallas kernels for 10%

profile of v1, /device:TPU:0, one launch (start us, length us, event | category | flops | bytes accessed | tf_op | source)
XLA Modules:
  0.0 935.5 jit_solution(2099677490303035966)
XLA Ops:
  39.7 26.3 %collective-permute-done.16 = bf16[64,2048]{1,0:T(8,128)(2,1)S(1)} collective-permute-done((bf16[64,2048]{1,0:T(8,128)(2,1)}, bf16[64,2048]{1,0:T(8,128)(2,1)S(1)}, u32[]{:S(2)}, u32[]{:S(2)}) %collective-permute-start.16) | collective-permute-done | bytes 262176 | tf_op jit(solution)/shard_map/ppermute | solution.py:38
  80.3 16.5 %collective-permute-done.4 = bf16[4,64,1536]{2,1,0:T(8,128)(2,1)S(1)} collective-permute-done((bf16[4,64,1536]{2,1,0:T(8,128)(2,1)S(1)}, bf16[4,64,1536]{2,1,0:T(8,128)(2,1)S(1)}, u32[]{:S(2)}, u32[]{:S(2)}) %collective-permute-start.4) | collective-permute-done | bytes 786464 | tf_op jit(solution)/shard_map/ppermute | solution.py:38
  103.8 23.1 %collective-permute-done.9 = bf16[4,64,2560]{2,1,0:T(8,128)(2,1)S(1)} collective-permute-done((bf16[4,64,2560]{2,1,0:T(8,128)(2,1)S(1)}, bf16[4,64,2560]{2,1,0:T(8,128)(2,1)S(1)}, u32[]{:S(2)}, u32[]{:S(2)}) %collective-permute-start.9) | collective-permute-done | bytes 1310752 | tf_op jit(solution)/shard_map/ppermute | solution.py:38
  142.8 15.5 %shard_map.263 = (bf16[1024,512]{1,0:T(8,128)(2,1)}, f32[4,2,1024]{2,1,0:T(2,128)}) custom-call(bf16[1024,512]{1,0:T(8,128)(2,1)} %add_convert_fusion.8.q_ref, bf16[1024,512]{1,0:T(8,128)(2,1)} %convolution_convert_fusion.15.k_ref, bf16[1024,512]{1,0:T(8,128)(2,1)} %add_convert_fusion.7.v_ref, s32[1024,1]{1,0:T(8,128)} %copy.39.row_ref.col_ref, ...), custom_call_target="tpu_custom_call" | custom-call | flops 8589934592 | bytes 4194304 | tf_op jit(solution)/shard_map/pallas_call | solution.py:214
  158.3 33.1 %collective-permute-done.10 = bf16[4,2,64,2560]{3,2,1,0:T(8,128)(2,1)} collective-permute-done((bf16[4,2,64,2560]{3,2,1,0:T(8,128)(2,1)}, bf16[4,2,64,2560]{3,2,1,0:T(8,128)(2,1)}, u32[]{:S(2)}, u32[]{:S(2)}) %collective-permute-start.10) | collective-permute-done | bytes 2621472 | tf_op jit(solution)/shard_map/ppermute | solution.py:38
  205.6 10.3 %collective-permute-done.22 = bf16[128,2048]{1,0:T(8,128)(2,1)S(1)} collective-permute-done((bf16[128,2048]{1,0:T(8,128)(2,1)}, bf16[128,2048]{1,0:T(8,128)(2,1)S(1)}, u32[]{:S(2)}, u32[]{:S(2)}) %collective-permute-start.22) | collective-permute-done | bytes 524320 | tf_op jit(solution)/shard_map/ppermute | solution.py:58
  228.0 12.1 %shard_map.264 = (bf16[1024,512]{1,0:T(8,128)(2,1)}, f32[4,2,1024]{2,1,0:T(2,128)}) custom-call(bf16[1024,512]{1,0:T(8,128)(2,1)} %add_convert_fusion.6.q_ref, bf16[512,512]{1,0:T(8,128)(2,1)} %convolution_convert_fusion.18.k_ref, bf16[512,512]{1,0:T(8,128)(2,1)} %fusion.31.v_ref, s32[1024,1]{1,0:T(8,128)} %copy.39.row_ref.col_ref, s32[1,512]{1,0:T(1,128)} %col_ref.3), custom_call_target="tpu_custom_call" | custom-call | flops 4294967296 | bytes 3145728 | tf_op jit(solution)/shard_map/pallas_call | solution.py:214
  252.6 17.3 %collective-permute-done.20 = bf16[4,128,2048]{2,1,0:T(8,128)(2,1)} collective-permute-done((bf16[4,128,2048]{2,1,0:T(8,128)(2,1)}, bf16[4,128,2048]{2,1,0:T(8,128)(2,1)}, u32[]{:S(2)}, u32[]{:S(2)}) %collective-permute-start.20) | collective-permute-done | bytes 2097184 | tf_op jit(solution)/shard_map/ppermute | solution.py:38
  277.8 35.8 %collective-permute-done.25 = bf16[4,128,2048]{2,1,0:T(8,128)(2,1)S(1)} collective-permute-done((bf16[4,128,2048]{2,1,0:T(8,128)(2,1)S(1)}, bf16[4,128,2048]{2,1,0:T(8,128)(2,1)S(1)}, u32[]{:S(2)}, u32[]{:S(2)}) %collective-permute-start.25) | collective-permute-done | bytes 2097184 | tf_op jit(solution)/shard_map/ppermute | solution.py:38
  320.9 18.4 %shard_map.265 = (bf16[1024,2048]{1,0:T(8,128)(2,1)}, bf16[1024,2048]{1,0:T(8,128)(2,1)}) custom-call(bf16[1024,1024]{1,0:T(8,128)(2,1)} %get-tuple-element.139.x_ref, bf16[1024,1024]{1,0:T(8,128)(2,1)} %get-tuple-element.140.g_ref, bf16[1024,2048]{1,0:T(8,128)(2,1)} %bitcast.351, bf16[1024,2048]{1,0:T(8,128)(2,1)} %bitcast.355, f32[1,2048]{1,0:T(1,128)} %bitcast.409), custom_call_target="tpu_custom_call" | custom-call | flops 8589934592 | bytes 20971520 | tf_op jit(solution)/shard_map/pallas_call | solution.py:286
  375.3 18.6 %shard_map.266 = (bf16[1024,2048]{1,0:T(8,128)(2,1)}, bf16[1024,2048]{1,0:T(8,128)(2,1)}) custom-call(bf16[1024,1024]{1,0:T(8,128)(2,1)} %get-tuple-element.137.x_ref, bf16[1024,1024]{1,0:T(8,128)(2,1)} %get-tuple-element.138.g_ref, bf16[1024,2048]{1,0:T(8,128)(2,1)} %bitcast.352, bf16[1024,2048]{1,0:T(8,128)(2,1)} %bitcast.356, f32[1,2048]{1,0:T(1,128)} %bitcast.410), custom_call_target="tpu_custom_call" | custom-call | flops 8589934592 | bytes 20971520 | tf_op jit(solution)/shard_map/pallas_call | solution.py:286
  420.2 10.0 %add_convert_fusion = bf16[1024,2048]{1,0:T(8,128)(2,1)} fusion(f32[1024,2048]{1,0:T(8,128)} %fusion.75, bf16[1024,2048]{1,0:T(8,128)(2,1)} %get-tuple-element.31, bf16[512,1024]{1,0:T(8,128)(2,1)S(1)} %copy-done.38, bf16[512,1024]{1,0:T(8,128)(2,1)S(1)} %copy-done.36), kind=kOutput, calls=%fused_computation | convolution fusion | flops 4303355904 | bytes 18874368 | tf_op jit(solution)/shard_map/dot_general | solution.py:21
  437.3 8.6 collective-permute-done.35
  448.3 18.9 %collective-permute-done.32 = bf16[512,1024]{1,0:T(8,128)(2,1)} collective-permute-done((bf16[512,1024]{1,0:T(8,128)(2,1)}, bf16[512,1024]{1,0:T(8,128)(2,1)}, u32[]{:S(2)}, u32[]{:S(2)}) %collective-permute-start.32) | collective-permute-done | bytes 1048608 | tf_op jit(solution)/shard_map/ppermute | solution.py:38
  478.4 32.1 %collective-permute-done.55 = bf16[4,128,2048]{2,1,0:T(8,128)(2,1)S(1)} collective-permute-done((bf16[4,128,2048]{2,1,0:T(8,128)(2,1)S(1)}, bf16[4,128,2048]{2,1,0:T(8,128)(2,1)S(1)}, u32[]{:S(2)}, u32[]{:S(2)}) %collective-permute-start.55) | collective-permute-done | bytes 2097184 | tf_op jit(solution)/shard_map/ppermute | solution.py:38
  513.3 28.0 %collective-permute-done.52 = bf16[128,2048]{1,0:T(8,128)(2,1)S(1)} collective-permute-done((bf16[128,2048]{1,0:T(8,128)(2,1)S(1)}, bf16[128,2048]{1,0:T(8,128)(2,1)S(1)}, u32[]{:S(2)}, u32[]{:S(2)}) %collective-permute-start.52) | collective-permute-done | bytes 524320 | tf_op jit(solution)/shard_map/ppermute | solution.py:70
  542.2 26.1 %collective-permute-done.57 = bf16[128,2048]{1,0:T(8,128)(2,1)S(1)} collective-permute-done((bf16[128,2048]{1,0:T(8,128)(2,1)S(1)}, bf16[128,2048]{1,0:T(8,128)(2,1)S(1)}, u32[]{:S(2)}, u32[]{:S(2)}) %collective-permute-start.57) | collective-permute-done | bytes 524320 | tf_op jit(solution)/shard_map/ppermute | solution.py:70
  579.7 21.8 %shard_map.267 = (bf16[1024,512]{1,0:T(8,128)(2,1)}, bf16[512,512]{1,0:T(8,128)(2,1)}, bf16[512,512]{1,0:T(8,128)(2,1)}) custom-call(bf16[1024,512]{1,0:T(8,128)(2,1)} %add_convert_fusion.6.q_ref, bf16[512,512]{1,0:T(8,128)(2,1)} %convolution_convert_fusion.18.k_ref, bf16[512,512]{1,0:T(8,128)(2,1)} %fusion.31.v_ref, ...), custom_call_target="tpu_custom_call" | custom-call | flops 10737418240 | bytes 3145728 | tf_op jit(solution)/shard_map/pallas_call | solution.py:234
  641.9 28.0 %shard_map.268 = (bf16[1024,512]{1,0:T(8,128)(2,1)}, bf16[1024,512]{1,0:T(8,128)(2,1)}, bf16[1024,512]{1,0:T(8,128)(2,1)}) custom-call(bf16[1024,512]{1,0:T(8,128)(2,1)} %add_convert_fusion.8.q_ref, bf16[1024,512]{1,0:T(8,128)(2,1)} %convolution_convert_fusion.15.k_ref, bf16[1024,512]{1,0:T(8,128)(2,1)} %add_convert_fusion.7.v_ref, ...), custom_call_target="tpu_custom_call" | custom-call | flops 21474836480 | bytes 4194304 | tf_op jit(solution)/shard_map/pallas_call | solution.py:234
  697.9 21.6 %collective-permute-done.46 = bf16[4,64,2048]{2,1,0:T(8,128)(2,1)S(1)} collective-permute-done((bf16[4,64,2048]{2,1,0:T(8,128)(2,1)S(1)}, bf16[4,64,2048]{2,1,0:T(8,128)(2,1)S(1)}, u32[]{:S(2)}, u32[]{:S(2)}) %collective-permute-start.46) | collective-permute-done | bytes 1048608 | tf_op jit(solution)/shard_map/ppermute | solution.py:38
  729.1 17.7 %collective-permute-done.48 = bf16[64,2048]{1,0:T(8,128)(2,1)} collective-permute-done((bf16[64,2048]{1,0:T(8,128)(2,1)}, bf16[64,2048]{1,0:T(8,128)(2,1)}, u32[]{:S(2)}, u32[]{:S(2)}) %collective-permute-start.48) | collective-permute-done | bytes 262176 | tf_op jit(solution)/shard_map/ppermute | solution.py:70
  760.5 11.7 %collective-permute-done.40 = bf16[4,2,64,2048]{3,2,1,0:T(8,128)(2,1)S(1)} collective-permute-done((bf16[4,2,64,2048]{3,2,1,0:T(8,128)(2,1)}, bf16[4,2,64,2048]{3,2,1,0:T(8,128)(2,1)S(1)}, u32[]{:S(2)}, u32[]{:S(2)}) %collective-permute-start.40) | collective-permute-done | bytes 2097184 | tf_op jit(solution)/shard_map/ppermute | solution.py:38
  778.9 115.2 %all-reduce.2.cloned.1.call-done = f32[21504]{0:T(1024)} async-done(((f32[21504]{0:T(1024)}), f32[21504]{0:T(1024)}) %all-reduce.2.cloned.1.call-update) | async-done | bytes 86032 | tf_op jit(solution)/shard_map/psum | solution.py:521
  912.6 14.2 %collective-permute-done.43 = bf16[64,2048]{1,0:T(8,128)(2,1)S(1)} collective-permute-done((bf16[64,2048]{1,0:T(8,128)(2,1)S(1)}, bf16[64,2048]{1,0:T(8,128)(2,1)S(1)}, u32[]{:S(2)}, u32[]{:S(2)}) %collective-permute-start.43) | collective-permute-done | bytes 262176 | tf_op jit(solution)/shard_map/ppermute | solution.py:70
  (520 shorter events, 338.6 us)
Async XLA Ops:
  7.2 886.9 %all-reduce.2.cloned.1.call-start = ((), (), s32[]{:S(2)}) async-start(), calls=%async_computation | async-start | bytes 172032 | tf_op jit(solution)/shard_map/psum | solution.py:521
  21.3 52.5 %collective-permute-start.6 = (bf16[64,2560]{1,0:T(8,128)(2,1)}, bf16[64,2560]{1,0:T(8,128)(2,1)}, u32[]{:S(2)}, u32[]{:S(2)}) collective-permute-start(bf16[64,2560]{1,0:T(8,128)(2,1)} %bitcast_dynamic-update-slice_fusion.16), channel_id=1, source_target_pairs={{0,8},{8,16},{16,24},{24,0},{1,9},{9,17},{17,25},{25,1},{2,10},{10... | collective-permute-start | bytes 983048 | tf_op jit(solution)/shard_map/ppermute | solution.py:58
  22.0 53.6 %collective-permute-start.7 = (bf16[64,2560]{1,0:T(8,128)(2,1)}, bf16[64,2560]{1,0:T(8,128)(2,1)}, u32[]{:S(2)}, u32[]{:S(2)}) collective-permute-start(bf16[64,2560]{1,0:T(8,128)(2,1)} %bitcast_dynamic-update-slice_fusion.16), channel_id=1, source_target_pairs={{0,16},{8,24},{16,0},{24,8},{1,17},{9,25},{17,1},{25,9},{2,18},{10... | collective-permute-start | bytes 983048 | tf_op jit(solution)/shard_map/ppermute | solution.py:58
  32.8 44.1 %collective-permute-start.8 = (bf16[64,2560]{1,0:T(8,128)(2,1)}, bf16[64,2560]{1,0:T(8,128)(2,1)S(1)}, u32[]{:S(2)}, u32[]{:S(2)}) collective-permute-start(bf16[64,2560]{1,0:T(8,128)(2,1)} %bitcast_dynamic-update-slice_fusion.16), channel_id=1, source_target_pairs={{0,24},{8,0},{16,8},{24,16},{1,25},{9,1},{17,9},{25,17},{2,26},{10... | collective-permute-start | bytes 983048 | tf_op jit(solution)/shard_map/ppermute | solution.py:58
  36.6 184.5 %collective-permute-start.29 = (bf16[512,1024]{1,0:T(8,128)(2,1)}, bf16[512,1024]{1,0:T(8,128)(2,1)}, u32[]{:S(2)}, u32[]{:S(2)}) collective-permute-start(bf16[512,1024]{1,0:T(8,128)(2,1)} %bitcast.44), channel_id=1, source_target_pairs={{0,2},{2,0},{1,3},{3,1},{4,6},{6,4},{5,7},{7,5},{8,10},{10,8},{9,1... | collective-permute-start | bytes 3145736 | tf_op jit(solution)/shard_map/ppermute | solution.py:38
  72.6 174.9 %collective-permute-start.15 = (bf16[512,1024]{1,0:T(8,128)(2,1)}, bf16[512,1024]{1,0:T(8,128)(2,1)}, u32[]{:S(2)}, u32[]{:S(2)}) collective-permute-start(bf16[512,1024]{1,0:T(8,128)(2,1)} %bitcast.44), channel_id=1, source_target_pairs={{0,1},{1,0},{2,3},{3,2},{4,5},{5,4},{6,7},{7,6},{8,9},{9,8},{10,11... | collective-permute-start | bytes 3145736 | tf_op jit(solution)/shard_map/ppermute | solution.py:38
  78.6 118.4 %collective-permute-start.17 = (bf16[128,2048]{1,0:T(8,128)(2,1)}, bf16[128,2048]{1,0:T(8,128)(2,1)}, u32[]{:S(2)}, u32[]{:S(2)}) collective-permute-start(bf16[128,2048]{1,0:T(8,128)(2,1)} %pad_maximum_fusion.18), channel_id=1, source_target_pairs={{0,8},{8,16},{16,24},{24,0},{1,9},{9,17},{17,25},{25,1},{2,10},{10... | collective-permute-start | bytes 1572872 | tf_op jit(solution)/shard_map/ppermute | solution.py:58
  126.9 72.1 %collective-permute-start.18 = (bf16[128,2048]{1,0:T(8,128)(2,1)}, bf16[128,2048]{1,0:T(8,128)(2,1)}, u32[]{:S(2)}, u32[]{:S(2)}) collective-permute-start(bf16[128,2048]{1,0:T(8,128)(2,1)} %pad_maximum_fusion.18), channel_id=1, source_target_pairs={{0,16},{8,24},{16,0},{24,8},{1,17},{9,25},{17,1},{25,9},{2,18},{10... | collective-permute-start | bytes 1572872 | tf_op jit(solution)/shard_map/ppermute | solution.py:58
  134.1 57.3 %collective-permute-start.10 = (bf16[4,2,64,2560]{3,2,1,0:T(8,128)(2,1)}, bf16[4,2,64,2560]{3,2,1,0:T(8,128)(2,1)}, u32[]{:S(2)}, u32[]{:S(2)}) collective-permute-start(bf16[4,2,64,2560]{3,2,1,0:T(8,128)(2,1)} %pad_maximum_fusion.6), channel_id=1, source_target_pairs={{0,2},{2,0},{1,3},{3,1},{4,6},{6,4},{5,7},{7,5},{8,10},{10,8},{9,1... | collective-permute-start | bytes 7864328 | tf_op jit(solution)/shard_map/ppermute | solution.py:38
  221.1 48.8 %collective-permute-start.20 = (bf16[4,128,2048]{2,1,0:T(8,128)(2,1)}, bf16[4,128,2048]{2,1,0:T(8,128)(2,1)}, u32[]{:S(2)}, u32[]{:S(2)}) collective-permute-start(bf16[4,128,2048]{2,1,0:T(8,128)(2,1)} %bitcast_dynamic-update-slice_fusion.4), channel_id=1, source_target_pairs={{0,4},{4,0},{1,5},{5,1},{2,6},{6,2},{3,7},{7,3},{8,12},{12,8},{9,1... | collective-permute-start | bytes 6291464 | tf_op jit(solution)/shard_map/ppermute | solution.py:38
  245.9 67.7 %collective-permute-start.25 = (bf16[4,128,2048]{2,1,0:T(8,128)(2,1)S(1)}, bf16[4,128,2048]{2,1,0:T(8,128)(2,1)S(1)}, u32[]{:S(2)}, u32[]{:S(2)}) collective-permute-start(bf16[4,128,2048]{2,1,0:T(8,128)(2,1)S(1)} %bitcast_dynamic-update-slice_fusion), channel_id=1, source_target_pairs={{0,4},{4,0},{1,5},{5,1},{2,6},{6,2},{3,7},{7,3},{8,12},{12,8},{9,1... | collective-permute-start | bytes 6291464 | tf_op jit(solution)/shard_map/ppermute | solution.py:38
  316.2 45.2 %collective-permute-start.27 = (bf16[512,1024]{1,0:T(8,128)(2,1)}, bf16[512,1024]{1,0:T(8,128)(2,1)}, u32[]{:S(2)}, u32[]{:S(2)}) collective-permute-start(bf16[512,1024]{1,0:T(8,128)(2,1)} %add_convert_fusion.5), channel_id=1, source_target_pairs={{0,2},{2,0},{1,3},{3,1},{4,6},{6,4},{5,7},{7,5},{8,10},{10,8},{9,1... | collective-permute-start | bytes 3145736 | tf_op jit(solution)/shard_map/ppermute | solution.py:38
  356.6 79.2 %collective-permute-start.33 = (bf16[512,1024]{1,0:T(8,128)(2,1)}, bf16[512,1024]{1,0:T(8,128)(2,1)S(1)}, u32[]{:S(2)}, u32[]{:S(2)}) collective-permute-start(bf16[512,1024]{1,0:T(8,128)(2,1)} %dynamic-slice_bitcast_fusion.7), channel_id=1, source_target_pairs={{0,1},{1,0},{2,3},{3,2},{4,5},{5,4},{6,7},{7,6},{8,9},{9,8},{10,11... | collective-permute-start | bytes 3145736 | tf_op jit(solution)/shard_map/ppermute | solution.py:38
  363.0 85.3 %collective-permute-start.26 = (bf16[512,1024]{1,0:T(8,128)(2,1)}, bf16[512,1024]{1,0:T(8,128)(2,1)}, u32[]{:S(2)}, u32[]{:S(2)}) collective-permute-start(bf16[512,1024]{1,0:T(8,128)(2,1)} %dynamic-slice_bitcast_fusion.9), channel_id=1, source_target_pairs={{0,1},{1,0},{2,3},{3,2},{4,5},{5,4},{6,7},{7,6},{8,9},{9,8},{10,11... | collective-permute-start | bytes 3145736 | tf_op jit(solution)/shard_map/ppermute | solution.py:38
  417.7 55.4 %collective-permute-start.50 = (bf16[4,128,2048]{2,1,0:T(8,128)(2,1)}, bf16[4,128,2048]{2,1,0:T(8,128)(2,1)}, u32[]{:S(2)}, u32[]{:S(2)}) collective-permute-start(bf16[4,128,2048]{2,1,0:T(8,128)(2,1)} %dynamic-slice_bitcast_fusion.1), channel_id=1, source_target_pairs={{0,4},{4,0},{1,5},{5,1},{2,6},{6,2},{3,7},{7,3},{8,12},{12,8},{9,1... | collective-permute-start | bytes 6291464 | tf_op jit(solution)/shard_map/ppermute | solution.py:38
  435.7 74.7 %collective-permute-start.55 = (bf16[4,128,2048]{2,1,0:T(8,128)(2,1)S(1)}, bf16[4,128,2048]{2,1,0:T(8,128)(2,1)S(1)}, u32[]{:S(2)}, u32[]{:S(2)}) collective-permute-start(bf16[4,128,2048]{2,1,0:T(8,128)(2,1)S(1)} %dynamic-slice_bitcast_fusion), channel_id=1, source_target_pairs={{0,4},{4,0},{1,5},{5,1},{2,6},{6,2},{3,7},{7,3},{8,12},{12,8},{9,1... | collective-permute-start | bytes 6291464 | tf_op jit(solution)/shard_map/ppermute | solution.py:38
  472.9 104.3 %collective-permute-start.36 = (bf16[512,1024]{1,0:T(8,128)(2,1)S(1)}, bf16[512,1024]{1,0:T(8,128)(2,1)S(1)}, u32[]{:S(2)}, u32[]{:S(2)}) collective-permute-start(bf16[512,1024]{1,0:T(8,128)(2,1)S(1)} %get-tuple-element.71), channel_id=1, source_target_pairs={{0,1},{1,0},{2,3},{3,2},{4,5},{5,4},{6,7},{7,6},{8,9},{9,8},{10,11... | collective-permute-start | bytes 3145736 | tf_op jit(solution)/shard_map/ppermute | solution.py:38
  477.2 64.1 %collective-permute-start.52 = (bf16[128,2048]{1,0:T(8,128)(2,1)S(1)}, bf16[128,2048]{1,0:T(8,128)(2,1)S(1)}, u32[]{:S(2)}, u32[]{:S(2)}) collective-permute-start(bf16[128,2048]{1,0:T(8,128)(2,1)S(1)} %get-tuple-element.81), channel_id=1, source_target_pairs={{0,16},{8,24},{16,0},{24,8},{1,17},{9,25},{17,1},{25,9},{2,18},{10... | collective-permute-start | bytes 1572872 | tf_op jit(solution)/shard_map/ppermute | solution.py:70
  477.9 63.4 %collective-permute-start.51 = (bf16[128,2048]{1,0:T(8,128)(2,1)S(1)}, bf16[128,2048]{1,0:T(8,128)(2,1)S(1)}, u32[]{:S(2)}, u32[]{:S(2)}) collective-permute-start(bf16[128,2048]{1,0:T(8,128)(2,1)S(1)} %get-tuple-element.79), channel_id=1, source_target_pairs={{0,8},{8,16},{16,24},{24,0},{1,9},{9,17},{17,25},{25,1},{2,10},{10... | collective-permute-start | bytes 1572872 | tf_op jit(solution)/shard_map/ppermute | solution.py:70
  512.4 56.0 %collective-permute-start.57 = (bf16[128,2048]{1,0:T(8,128)(2,1)S(1)}, bf16[128,2048]{1,0:T(8,128)(2,1)S(1)}, u32[]{:S(2)}, u32[]{:S(2)}) collective-permute-start(bf16[128,2048]{1,0:T(8,128)(2,1)S(1)} %get-tuple-element.78), channel_id=1, source_target_pairs={{0,16},{8,24},{16,0},{24,8},{1,17},{9,25},{17,1},{25,9},{2,18},{10... | collective-permute-start | bytes 1572872 | tf_op jit(solution)/shard_map/ppermute | solution.py:70
  625.4 65.4 %collective-permute-start.45 = (bf16[4,2,64,2048]{3,2,1,0:T(8,128)(2,1)}, bf16[4,2,64,2048]{3,2,1,0:T(8,128)(2,1)}, u32[]{:S(2)}, u32[]{:S(2)}) collective-permute-start(bf16[4,2,64,2048]{3,2,1,0:T(8,128)(2,1)} %dynamic-slice_bitcast_fusion.2), channel_id=1, source_target_pairs={{0,2},{2,0},{1,3},{3,1},{4,6},{6,4},{5,7},{7,5},{8,10},{10,8},{9,1... | collective-permute-start | bytes 6291464 | tf_op jit(solution)/shard_map/ppermute | solution.py:38
  676.5 73.0 %collective-permute-start.38 = (bf16[1024,1024]{1,0:T(8,128)(2,1)}, bf16[1024,1024]{1,0:T(8,128)(2,1)}, u32[]{:S(2)}, u32[]{:S(2)}) collective-permute-start(bf16[1024,1024]{1,0:T(8,128)(2,1)} %add_convert_fusion.2), channel_id=1, source_target_pairs={{0,1},{1,0},{2,3},{3,2},{4,5},{5,4},{6,7},{7,6},{8,9},{9,8},{10,11... | collective-permute-start | bytes 6291464 | tf_op jit(solution)/shard_map/ppermute | solution.py:38
  725.7 46.5 %collective-permute-start.40 = (bf16[4,2,64,2048]{3,2,1,0:T(8,128)(2,1)}, bf16[4,2,64,2048]{3,2,1,0:T(8,128)(2,1)S(1)}, u32[]{:S(2)}, u32[]{:S(2)}) collective-permute-start(bf16[4,2,64,2048]{3,2,1,0:T(8,128)(2,1)} %dynamic-slice_bitcast_fusion.3), channel_id=1, source_target_pairs={{0,2},{2,0},{1,3},{3,1},{4,6},{6,4},{5,7},{7,5},{8,10},{10,8},{9,1... | collective-permute-start | bytes 6291464 | tf_op jit(solution)/shard_map/ppermute | solution.py:38
  773.2 125.7 %collective-permute-start.41 = (bf16[4,64,2048]{2,1,0:T(8,128)(2,1)S(1)}, bf16[4,64,2048]{2,1,0:T(8,128)(2,1)}, u32[]{:S(2)}, u32[]{:S(2)}) collective-permute-start(bf16[4,64,2048]{2,1,0:T(8,128)(2,1)S(1)} %dynamic-slice_bitcast_fusion.5), channel_id=1, source_target_pairs={{0,4},{4,0},{1,5},{5,1},{2,6},{6,2},{3,7},{7,3},{8,12},{12,8},{9,1... | collective-permute-start | bytes 3145736 | tf_op jit(solution)/shard_map/ppermute | solution.py:38
  (142 other events, 2303.3 us)
Sparse Core Ops, SparseCore 0:
  775.6 118.4 all-reduce.1

commit v2 on v1

v2 whole, which is shorter than its diff:
```python
import functools
import math

import jax
import jax.numpy as jnp
from jax import lax
from jax.experimental import pallas as pl
from jax.experimental.pallas import tpu as pltpu
from jax.sharding import Mesh
from jax.sharding import PartitionSpec as P

HEAD = 64
PAIR = 2 * HEAD
F32 = jnp.float32
BF16 = jnp.bfloat16
VMEM_LIMIT = 56 * 1024 * 1024
MASKED = -1e30


def dot(left, right, left_dim, right_dim):
    return lax.dot_general(
        left, right, (((left_dim,), (right_dim,)), ((), ())), preferred_element_type=F32
    )


def normalize(values, gain_row, shift_row):
    average = jnp.mean(values, axis=-1, keepdims=True)
    centred = values - average
    spread = jnp.mean(centred * centred, axis=-1, keepdims=True)
    return centred * lax.rsqrt(spread + 1e-05) * gain_row + shift_row


def row_total(rows):
    return jnp.sum(rows.astype(F32), axis=0)


def after(values, *earlier):
    return lax.optimization_barrier((values, earlier))[0]


def swap(values, axis):
    return lax.ppermute(values, axis, [(0, 1), (1, 0)])


def join_pair(own, other, index, dim):
    size = own.shape[dim]
    whole = jnp.zeros(own.shape[:dim] + (2 * size,) + own.shape[dim + 1 :], own.dtype)
    whole = lax.dynamic_update_slice_in_dim(whole, own, index * size, dim)
    return lax.dynamic_update_slice_in_dim(whole, other, (1 - index) * size, dim)


def stack_pair(own, other, index, dim):
    return join_pair(jnp.expand_dims(own, dim), jnp.expand_dims(other, dim), index, dim)


AXES = ("zh", "zl", "y", "x")


class Gather:
    def __init__(self, shard, order, *earlier):
        shard = after(shard, *earlier) if earlier else shard
        self.blocks = shard.reshape((1, 1, 1, 1) + shard.shape)
        self.order = list(order)
        self.send()

    def send(self):
        self.axis = self.order.pop(0)
        if lax.axis_size(self.axis) == 2:
            self.got = swap(self.blocks, self.axis)
        else:
            dim = AXES.index(self.axis)
            self.got = lax.all_gather(self.blocks, self.axis, axis=dim, tiled=True)

    def parts(self, *earlier):
        got = after(self.got, *earlier) if earlier else self.got
        dim = AXES.index(self.axis)
        if lax.axis_size(self.axis) != 2:
            return [(got, dim, 0)]
        me = lax.axis_index(self.axis)
        return [(self.blocks, dim, me), (got, dim, 1 - me)]

    def join(self, *earlier):
        self.blocks = assemble([self], *earlier)
        return self.blocks

    def step(self, *earlier, first=()):
        blocks = self.join(*earlier)
        if first:
            self.blocks = after(blocks, *first)
        self.send()
        return blocks


def assemble(gathers, *earlier):
    pieces = [gather.parts(*earlier) for gather in gathers]
    if len(gathers) == 1 and len(pieces[0]) == 1:
        return pieces[0][0][0]
    shape = list(pieces[0][0][0].shape)
    for part in pieces[0][1:]:
        shape[part[1]] += part[0].shape[part[1]]
    shape[-1] = sum(piece[0][0].shape[-1] for piece in pieces)
    whole = jnp.zeros(shape, BF16)
    column = 0
    for piece in pieces:
        for block, dim, index in piece:
            start = [0] * len(shape)
            start[dim] = index * block.shape[dim]
            start[-1] = column
            whole = lax.dynamic_update_slice(whole, block, start)
        column += piece[0][0].shape[-1]
    return whole


class Scatter:
    def __init__(self, blocks, order):
        self.order = list(order)
        self.left = [axis for axis in AXES if axis in order]
        self.send(blocks)

    def send(self, blocks):
        axis = self.order.pop(0)
        dim = self.left.index(axis)
        self.left.pop(dim)
        if lax.axis_size(axis) == 2:
            self.keep, self.got = halve_send(blocks, axis, dim)
        else:
            self.keep = lax.psum_scatter(
                blocks.astype(F32), axis, scatter_dimension=dim, tiled=False
            )
            self.got = jnp.zeros((1,), F32)

    def step(self, *earlier):
        got = after(self.got, *earlier) if earlier else self.got
        total = self.keep.astype(F32) + got.astype(F32)
        if self.order:
            total = total.astype(BF16)
            self.send(total)
        return total


def line_total(values):
    if lax.axis_size("zh") != 2:
        return lax.psum(values, "zh")
    return values + swap(values, "zh")


def halve_send(blocks, axis, dim):
    me = lax.axis_index(axis)
    keep = lax.dynamic_index_in_dim(blocks, me, dim, False)
    send = lax.dynamic_index_in_dim(blocks, 1 - me, dim, False)
    return keep, swap(send, axis)


def halves(values, low):
    zero = jnp.zeros_like(values)
    return jnp.where(low, values, zero), jnp.where(low, zero, values)


def low_lanes():
    return lax.broadcasted_iota(jnp.int32, (1, PAIR), 1) < HEAD


def forward_kernel(causal, tile, q_ref, k_ref, v_ref, row_ref, col_ref, o_ref, log_ref):
    length, width = q_ref.shape[0], k_ref.shape[0]
    low = low_lanes()
    for number in range(length // tile):
        rows = pl.ds(number * tile, tile)
        q_parts = halves(q_ref[rows, :] * 0.125, low)
        spans = [(0, width)]
        if causal:
            spans = [(0, number * tile)] if number else []
            spans.append((number * tile, tile))
        allowed = []
        for start, size in spans:
            same = row_ref[rows, :] == col_ref[:, pl.ds(start, size)]
            if causal and start == number * tile:
                same = same & (
                    lax.broadcasted_iota(jnp.int32, (tile, size), 0)
                    >= lax.broadcasted_iota(jnp.int32, (tile, size), 1)
                )
            allowed.append(same)
        result = jnp.zeros((tile, PAIR), F32)
        tops, sums = [], []
        for half in range(2):
            scores = []
            for (start, size), same in zip(spans, allowed):
                part = dot(q_parts[half], k_ref[pl.ds(start, size), :], 1, 1)
                scores.append(jnp.where(same, part, MASKED))
            top = functools.reduce(
                jnp.maximum, [jnp.max(part, axis=1, keepdims=True) for part in scores]
            )
            summed = jnp.zeros((tile, 1), F32)
            for (start, size), part in zip(spans, scores):
                chance = jnp.exp(part - top)
                summed = summed + jnp.sum(chance, axis=1, keepdims=True)
                v_part = halves(v_ref[pl.ds(start, size), :], low)[half]
                result = result + dot(chance.astype(BF16), v_part, 1, 0)
            tops.append(top)
            sums.append(summed)
        total = jnp.where(low, sums[0], sums[1])
        o_ref[rows, :] = (result / total).astype(BF16)
        logs = jnp.where(low, tops[0], tops[1]) + jnp.log(total)
        flipped = logs.T
        log_ref[0, 0:1, rows] = flipped[0:1, :]
        log_ref[0, 1:2, rows] = flipped[HEAD : HEAD + 1, :]


def backward_kernel(
    causal,
    tile,
    columns,
    q_ref,
    k_ref,
    v_ref,
    o_ref,
    g_ref,
    log_ref,
    row_ref,
    col_ref,
    *outs,
):
    dq_ref, dkv_ref, dk_sum, dv_sum = outs[0], outs[-3], outs[-2], outs[-1]
    length, width = q_ref.shape[0], k_ref.shape[0]
    low = low_lanes()
    q_at, k_at, v_at = (
        pl.ds(pl.multiple_of(column + pl.program_id(0) * PAIR, PAIR), PAIR) for column in columns
    )
    dk_sum[...] = jnp.zeros_like(dk_sum)
    dv_sum[...] = jnp.zeros_like(dv_sum)
    for number in range(length // tile):
        rows = pl.ds(number * tile, tile)
        q_parts = halves(q_ref[rows, :] * 0.125, low)
        grad = g_ref[rows, :]
        g_parts = halves(grad, low)
        product = (grad.astype(F32) * o_ref[rows, :].astype(F32)).T
        deltas = [
            jnp.sum(product[:HEAD], axis=0, keepdims=True),
            jnp.sum(product[HEAD:], axis=0, keepdims=True),
        ]
        dq = jnp.zeros((tile, PAIR), F32)
        for other in range(number + 1 if causal else width // tile):
            cols = pl.ds(other * tile, tile)
            same = col_ref[cols, :] == row_ref[:, rows]
            if causal and other == number:
                same = same & (
                    lax.broadcasted_iota(jnp.int32, (tile, tile), 1)
                    >= lax.broadcasted_iota(jnp.int32, (tile, tile), 0)
                )
            key, value = k_ref[cols, :], v_ref[cols, :]
            k_parts = halves(key, low)
            dk = jnp.zeros((tile, PAIR), F32)
            dv = jnp.zeros((tile, PAIR), F32)
            for half in range(2):
                scores = jnp.where(same, dot(key, q_parts[half], 1, 1), MASKED)
                chance = jnp.exp(scores - log_ref[0, half : half + 1, rows])
                dv = dv + dot(chance.astype(BF16), g_parts[half], 1, 0)
                change = dot(value, g_parts[half], 1, 1)
                inner = (chance * (change - deltas[half])).astype(BF16)
                dk = dk + dot(inner, q_parts[half], 1, 0)
                dq = dq + dot(inner, k_parts[half], 0, 0)
            dk_sum[cols, :] += dk
            dv_sum[cols, :] += dv
        dq_ref[rows, q_at] = (dq * 0.125).astype(BF16)
    dkv_ref[:, k_at] = dk_sum[...].astype(BF16)
    dkv_ref[:, v_at] = dv_sum[...].astype(BF16)


SMALL_COST = pl.CostEstimate(flops=1024, bytes_accessed=1024, transcendentals=0)


def pair_at(size, first):
    return pl.BlockSpec((size, PAIR), lambda pair: (0, first + pair))


def fixed(shape):
    return pl.BlockSpec(shape, lambda pair: (0, 0))


def logs_at(length):
    return pl.BlockSpec((1, 2, length), lambda pair: (pair, 0, 0))


def attend(query_set, key_set, columns, features, row_docs, col_docs, causal):
    length, width = query_set.shape[0], key_set.shape[0]
    tile = min(256, length)
    return pl.pallas_call(
        functools.partial(forward_kernel, causal, tile),
        grid=(features // PAIR,),
        in_specs=[
            pair_at(length, columns[0] // PAIR),
            pair_at(width, columns[1] // PAIR),
            pair_at(width, columns[2] // PAIR),
            fixed((length, 1)),
            fixed((1, width)),
        ],
        out_specs=[pair_at(length, 0), logs_at(length)],
        out_shape=[
            jax.ShapeDtypeStruct((length, features), BF16),
            jax.ShapeDtypeStruct((features // PAIR, 2, length), F32),
        ],
        compiler_params=pltpu.CompilerParams(vmem_limit_bytes=VMEM_LIMIT),
        cost_estimate=SMALL_COST,
    )(query_set, key_set, key_set, row_docs[:, None], col_docs[None, :])


def attend_back(
    query_set, key_set, columns, features, result, grad, logs, row_docs, col_docs, causal
):
    length, width = query_set.shape[0], key_set.shape[0]
    tile = min(256, length, width)
    outs = [jax.ShapeDtypeStruct(query_set.shape, BF16)]
    if key_set is not query_set:
        outs.append(jax.ShapeDtypeStruct(key_set.shape, BF16))
    return pl.pallas_call(
        functools.partial(backward_kernel, causal, tile, columns),
        grid=(features // PAIR,),
        in_specs=[
            pair_at(length, columns[0] // PAIR),
            pair_at(width, columns[1] // PAIR),
            pair_at(width, columns[2] // PAIR),
            pair_at(length, 0),
            pair_at(length, 0),
            logs_at(length),
            fixed((1, length)),
            fixed((width, 1)),
        ],
        out_specs=[fixed(out.shape) for out in outs],
        out_shape=outs,
        scratch_shapes=[pltpu.VMEM((width, PAIR), F32), pltpu.VMEM((width, PAIR), F32)],
        compiler_params=pltpu.CompilerParams(vmem_limit_bytes=VMEM_LIMIT),
        cost_estimate=SMALL_COST,
    )(query_set, key_set, key_set, result, grad, logs, row_docs[None, :], col_docs[:, None])


def gelu_and_slope(values):
    tail = jnp.exp(values * values * -0.5)
    step = 1.0 / (1.0 + (0.3275911 * math.sqrt(0.5)) * jnp.abs(values))
    series = 1.061405429
    for factor in (-1.453152027, 1.421413741, -0.284496736, 0.254829592):
        series = series * step + factor
    outside = (0.5 * series) * step * tail
    below = jnp.where(values >= 0, 1.0 - outside, outside)
    return values * below, below + values * tail * (1.0 / math.sqrt(2.0 * math.pi))


def hidden_kernel(piece, x_ref, g_ref, up_ref, down_ref, bias_ref, act_ref, grad_ref):
    for number in range(x_ref.shape[0] // piece):
        rows = pl.ds(number * piece, piece)
        before = dot(x_ref[rows, :], up_ref[...], 1, 0) + bias_ref[...]
        act, slope = gelu_and_slope(before)
        act_ref[rows, :] = act.astype(BF16)
        raw = dot(g_ref[rows, :], down_ref[...], 1, 0)
        grad_ref[rows, :] = (raw * slope).astype(BF16)


def hidden_parts(normed, grad, up, down_rows, bias_row):
    rows, features = normed.shape
    hidden = up.shape[1]
    tile = min(512, hidden)
    whole = pl.BlockSpec((rows, features), lambda step: (0, 0))
    piece = lambda height: pl.BlockSpec((height, tile), lambda step: (0, step))
    return pl.pallas_call(
        functools.partial(hidden_kernel, min(256, rows)),
        grid=(hidden // tile,),
        in_specs=[whole, whole, piece(features), piece(features), piece(1)],
        out_specs=[piece(rows), piece(rows)],
        out_shape=[jax.ShapeDtypeStruct((rows, hidden), BF16)] * 2,
        compiler_params=pltpu.CompilerParams(vmem_limit_bytes=VMEM_LIMIT),
        cost_estimate=SMALL_COST,
    )(normed, grad, up, down_rows, bias_row)


def per_device(
    tokens,
    memory,
    segments,
    sources,
    gains,
    biases,
    head_biases,
    self_proj,
    self_out,
    cross_query,
    cross_kv,
    cross_out,
    up_weight,
    up_bias,
    down_weight,
    cotangent,
):
    at_x, at_y, at_core = (lax.axis_index(axis) for axis in ("x", "y", "core"))
    row_docs, col_docs = segments[0], sources[0]
    half_rows, features = tokens.shape[1:]
    width = self_out.shape[0]
    part_rows = self_out.shape[1]
    hidden_part = up_weight.shape[1] // 2
    chunk = hidden_part // 2

    def short(part):
        return part.astype(BF16)

    def own_rows(values):
        return lax.dynamic_slice_in_dim(values, at_core * half_rows, half_rows, 0)

    def core_join(own, other):
        return join_pair(own, other, at_core, 0)

    def summed(partial):
        brief = short(partial)
        return brief.astype(F32) + swap(brief, "core").astype(F32)

    def summed_rows(partial):
        brief = short(partial)
        keep, got = halve_send(brief.reshape((2, -1) + brief.shape[1:]), "core", 0)
        return keep.astype(F32) + got.astype(F32)

    first = jnp.concatenate([short(self_proj[number]) for number in range(3)], 1)
    second = jnp.concatenate([short(self_out).T, short(cross_query)], 1)
    third = jnp.concatenate([short(cross_kv[0]), short(cross_kv[1]), short(cross_out).T], 1)
    cut = first.shape[1] // 2
    line_first, x_first = ("zh", "zl", "y", "x"), ("x", "y", "zh", "zl")
    g_one = Gather(first[:, :cut], line_first)
    g_two = Gather(first[:, cut:], x_first)
    tokens_core = swap(tokens[0], "core")
    grad_mine = cotangent[0]

    def pair_rows(shard):
        keep = lax.dynamic_slice_in_dim(shard, at_x * hidden_part, hidden_part, 1)
        send = lax.dynamic_slice_in_dim(shard, (1 - at_x) * hidden_part, hidden_part, 1)
        return join_pair(keep, swap(send, "x"), at_x, 0)

    rows_in = core_join(tokens[0], tokens_core).astype(F32)
    norm_one, back_one = jax.vjp(normalize, rows_in, gains[0], biases[0])
    norm_one = short(norm_one)

    one = g_one.step()
    two = g_two.step()
    up_rows, down_part = (pair_rows(short(up_weight)), pair_rows(short(down_weight).T))
    hidden_rows = [up_rows[:, :chunk], up_rows[:, chunk:], down_part[:, :chunk], down_part[:, chunk:]]
    hidden_order = ("zh", "zl", "y")
    g_out = Gather(second, line_first, one)
    one = g_one.step()
    two = g_two.step()
    out = g_out.step(first=(one,))
    g_kv = Gather(third, line_first, out)
    memory_core = swap(after(memory[0], two), "core")
    one = g_one.step()
    out = g_out.step(first=(one,))
    kv = g_kv.step(first=(out,))
    two = g_two.step()
    kv = g_kv.step(two)
    w_first = assemble([g_one, g_two]).reshape(features, -1)
    g_up = Gather(hidden_rows[0], hidden_order, w_first)
    out = g_out.step(first=(w_first,))

    bias_first = jnp.concatenate([head_biases[0], jnp.zeros((width,), F32), head_biases[1]])
    qkv = short(dot(after(norm_one, out, kv), w_first, 1, 0) + bias_first)
    up_one = g_up.step(qkv)
    g_up_two = Gather(hidden_rows[1], hidden_order, up_one)
    kv = g_kv.step(qkv)

    self_columns, cross_columns = (0, width, 2 * width), (0, 0, width)
    attended, logs_self = attend(
        after(qkv, up_one, kv), qkv, self_columns, width, row_docs, row_docs, True
    )

    w_second = g_out.join(attended).reshape(features, -1)
    grad_core = swap(after(grad_mine, attended), "core")
    up_one = g_up.step(attended)
    up_two = g_up_two.step(attended)
    g_down = Gather(hidden_rows[2], hidden_order, up_two)
    w_out, w_cross_query = w_second[:, :width], w_second[:, width:]

    after_self = rows_in + summed(dot(after(attended, up_one, up_two), w_out, 1, 1)) + biases[1]
    norm_two, back_two = jax.vjp(normalize, after_self, gains[1], biases[2])
    norm_two = short(norm_two)
    up_two = g_up_two.step(norm_two)
    down_one = g_down.step(norm_two)
    g_down_two = Gather(hidden_rows[3], hidden_order, down_one)
    cross_queries = short(
        dot(after(norm_two, up_two, down_one), w_cross_query, 1, 0) + head_biases[2]
    )

    w_third = g_kv.join(cross_queries).reshape(features, -1)
    grad_theirs = swap(after(grad_mine, w_third), "x")
    w_cross_kv, w_cross_out = w_third[:, : 2 * width], w_third[:, 2 * width :]
    mem_rows = core_join(memory[0], memory_core)
    bias_kv = jnp.concatenate([jnp.zeros((width,), F32), head_biases[3]])
    cross_kvs = short(dot(mem_rows, w_cross_kv, 1, 0) + bias_kv)
    down_one = g_down.step(cross_kvs)
    down_two = g_down_two.step(cross_kvs)
    cross_attended, logs_cross = attend(
        after(cross_queries, down_one, down_two, g_up.got),
        cross_kvs,
        cross_columns,
        width,
        row_docs,
        col_docs,
        False,
    )
    down_two = g_down_two.step(cross_attended)
    after_cross = (
        after_self
        + summed(dot(after(cross_attended, down_two, g_up_two.got), w_cross_out, 1, 1))
        + biases[3]
    )
    after_cross_mine = own_rows(after_cross)
    norm_three, back_three = jax.vjp(normalize, after_cross_mine, gains[2], biases[4])
    norm_three = short(norm_three)
    norm_theirs = swap(norm_three, "x")
    norm_own = core_join(norm_three, swap(after(norm_three, grad_theirs), "core"))
    grad_own = core_join(grad_mine, grad_core)
    grad_other = core_join(grad_theirs, swap(grad_theirs, "core"))

    up = assemble([g_up, g_up_two]).reshape(features, hidden_part)
    down_rows = assemble([g_down, g_down_two], norm_three).reshape(features, hidden_part)
    bias_part = lax.dynamic_slice_in_dim(up_bias, at_x * hidden_part, hidden_part, 0)[None, :]

    act_own, hid_own = hidden_parts(norm_own, grad_own, up, down_rows, bias_part)
    norm_theirs = after(norm_theirs, act_own)
    norm_other = core_join(norm_theirs, swap(norm_theirs, "core"))
    act_other, hid_other = hidden_parts(norm_other, grad_other, up, down_rows, bias_part)

    back_own = dot(hid_own, up, 1, 1)
    back_other = dot(hid_other, up, 1, 1)
    part_other = summed_rows(back_other)
    theirs_three = swap(short(part_other), "x")
    part_own = summed_rows(back_own)

    hidden_way, all_way = ("y", "zl", "zh"), ("x", "y", "zl", "zh")

    def scatter(grad, way):
        return Scatter(grad.reshape(up_blocks[: len(way)] + (-1, grad.shape[1])), way)

    up_blocks = tuple(lax.axis_size(axis) for axis in AXES)

    chunks = []
    ready = [part_own]
    for left_own, left_other, right_own, right_other in (
        (grad_own, grad_other, act_own, act_other),
        (norm_own, norm_other, hid_own, hid_other),
    ):
        for half in range(2):
            columns = slice(half * chunk, (half + 1) * chunk)
            grad = short(
                dot(after(left_own, *ready), right_own[:, columns], 0, 0)
                + dot(after(left_other, *ready), right_other[:, columns], 0, 0)
            )
            if len(chunks) > 1:
                grad = after(grad, chunks[len(chunks) - 2].got)
            chunks.append(scatter(grad, hidden_way))
            ready = [grad]
    one, two, three, four = chunks

    moved = one.step(*ready)
    fed_other = summed_rows(dot(after(act_other, moved), down_rows, 1, 1))
    fed_own = dot(after(act_own, moved, fed_other), down_rows, 1, 1)
    d_norm_three = part_own + after(theirs_three, fed_own).astype(F32)
    grad_rows = grad_mine.astype(F32)
    d_bias_five = row_total(grad_rows)
    back_rows, d_gain_two, d_bias_four = back_three(d_norm_three)
    d_cross_res = grad_rows + back_rows
    d_bias_three = row_total(d_cross_res)
    res_mine = short(d_cross_res)
    moved = [one.step(res_mine), two.step(res_mine)]
    res_rows = core_join(res_mine, swap(res_mine, "core"))
    fed_theirs = swap(short(after(fed_other, res_mine)), "x")
    fed_own = summed_rows(fed_own)
    d_up_bias = row_total(hid_own) + row_total(hid_other)

    def exchange(rows):
        rows = rows.reshape(2, part_rows, -1)
        keep = lax.dynamic_index_in_dim(rows, at_x, 0, False)
        send = lax.dynamic_index_in_dim(rows, 1 - at_x, 0, False).astype(BF16)
        return keep, swap(send, "x")

    d_cross_att = short(dot(after(res_rows, *moved), w_cross_out, 1, 0))
    d_cross_out = scatter(short(dot(res_rows, cross_attended, 0, 0)), all_way)
    moved = [two.step(d_cross_att), three.step(d_cross_att)]
    one = exchange(one.step(d_cross_att))
    cq_grad, ckv_grad = attend_back(
        cross_queries,
        cross_kvs,
        cross_columns,
        width,
        cross_attended,
        after(d_cross_att, *moved),
        logs_cross,
        row_docs,
        col_docs,
        False,
    )
    d_norm_two = summed(dot(cq_grad, w_cross_query, 1, 1))
    d_memory_part = dot(ckv_grad, w_cross_kv, 1, 1)
    moved = [four.step(cq_grad), three.step(cq_grad), d_cross_out.step(cq_grad)]
    d_cross_kv = scatter(short(dot(after(mem_rows, *moved), ckv_grad, 0, 0)), all_way)
    d_cross_query = scatter(short(dot(norm_two, cq_grad, 0, 0)), all_way)
    two = exchange(two.step(cq_grad))
    d_memory = short(summed_rows(d_memory_part))
    back_rows, d_gain_one, d_bias_two = back_two(d_norm_two)
    d_self_res = res_rows.astype(F32) + back_rows
    d_bias_one = row_total(d_self_res)
    self_rows = short(d_self_res)

    d_attended = short(dot(self_rows, w_out, 1, 0))
    d_self_out = scatter(short(dot(self_rows, attended, 0, 0)), all_way)
    moved = [four.step(d_attended), d_cross_out.step(d_attended), d_cross_kv.step(d_attended)]
    three = exchange(three.step(d_attended))
    (qkv_grad,) = attend_back(
        qkv,
        qkv,
        self_columns,
        width,
        attended,
        after(d_attended, *moved),
        logs_self,
        row_docs,
        row_docs,
        True,
    )
    moved = [
        d_cross_query.step(qkv_grad),
        d_self_out.step(qkv_grad),
        d_cross_kv.step(qkv_grad),
        d_cross_out.step(qkv_grad),
    ]
    four = exchange(four.step(qkv_grad))
    cut = 3 * width // 2
    grad_first = short(dot(after(norm_one, *moved[:2]), qkv_grad[:, :cut], 0, 0))
    d_self_one = scatter(grad_first, all_way)
    grad_first = short(dot(after(norm_one, grad_first), qkv_grad[:, cut:], 0, 0))
    d_self_two = scatter(grad_first, ("y", "x", "zl", "zh"))
    d_norm_one = summed_rows(dot(after(qkv_grad, grad_first), w_first, 1, 1))
    layer_out = short(after_cross_mine + fed_own + after(fed_theirs, grad_first).astype(F32) + biases[5])
    moved = [
        d_self_one.step(d_norm_one),
        d_self_two.step(d_norm_one),
        d_cross_query.step(d_norm_one),
        d_self_out.step(d_norm_one),
    ]
    _, back_one = jax.vjp(normalize, own_rows(rows_in), gains[0], biases[0])
    back_rows, d_gain_zero, d_bias_zero = back_one(after(d_norm_one, *moved))
    d_tokens = short(own_rows(d_self_res) + back_rows)

    qkv_total = row_total(qkv_grad)
    head_rows = jnp.stack(
        [
            qkv_total[:width],
            qkv_total[2 * width :],
            row_total(cq_grad),
            row_total(ckv_grad)[width:],
        ]
    )
    head_place = jnp.zeros((4, 2, width), F32)
    head_place = lax.dynamic_update_slice(head_place, head_rows[:, None], (0, at_core, 0))
    bias_place = jnp.zeros((2, 2, hidden_part), F32)
    bias_place = lax.dynamic_update_slice(bias_place, d_up_bias[None, None], (at_core, at_x, 0))
    small = jnp.concatenate(
        [
            jnp.stack(
                [
                    d_gain_zero,
                    d_gain_one * 0.5,
                    d_gain_two,
                    d_bias_zero,
                    d_bias_one * 0.5,
                    d_bias_two * 0.5,
                    d_bias_three,
                    d_bias_four,
                    d_bias_five,
                ]
            ),
            head_place.reshape(-1, features),
            bias_place.reshape(-1, features),
        ]
    )
    for axis in ("core", "x", "y", "zl"):
        small = small + swap(small, axis)
    small = line_total(small)
    head_place = small[9 : 9 + head_place.size // features].reshape(head_place.shape)
    bias_place = small[9 + head_place.size // features :].reshape(2, 2 * hidden_part)
    d_head_biases = lax.dynamic_index_in_dim(head_place, at_core, 1, False)
    d_up_bias = lax.dynamic_index_in_dim(bias_place, at_core, 0, False)

    d_self_one.step(d_tokens)
    d_self_two.step(d_tokens)
    d_cross_kv.step(d_tokens)
    d_cross_out = d_cross_out.step(d_tokens)
    d_cross_query.step(d_tokens)
    d_self_out.step(d_tokens)
    d_self_one.step()
    d_self_two.step()
    d_cross_kv = d_cross_kv.step()
    d_cross_query = d_cross_query.step()
    d_self_out = d_self_out.step()
    d_self_proj = jnp.concatenate([d_self_one.step(), d_self_two.step()], 1)

    def joined(left, right):
        return join_pair(
            jnp.concatenate([left[0], right[0]], 1),
            jnp.concatenate([left[1], right[1]], 1).astype(F32),
            at_x,
            1,
        )

    return (
        layer_out[None],
        d_tokens[None],
        d_memory[None],
        small[:3],
        small[3:9],
        d_head_biases,
        jnp.stack([d_self_proj[:, number * width : (number + 1) * width] for number in range(3)]),
        d_self_out.T,
        d_cross_query,
        jnp.stack([d_cross_kv[:, :width], d_cross_kv[:, width:]]),
        d_cross_out.T,
        joined(three, four),
        d_up_bias,
        joined(one, two).T,
    )


def solution(mesh):
    members, cores = mesh.devices.shape
    parts = Mesh(mesh.devices.reshape(members // 8, 2, 2, 2, cores), AXES + ("core",))
    dp = AXES
    in_specs = (
        P(dp, "core", None),
        P(dp, "core", None),
        P(dp, None),
        P(dp, None),
        P(),
        P(),
        P(None, "core"),
        P(None, dp, "core"),
        P("core", dp),
        P(dp, "core"),
        P(None, dp, "core"),
        P("core", dp),
        P(dp, "core"),
        P("core"),
        P("core", dp),
        P(dp, "core", None),
    )
    out_specs = (
        P(dp, "core", None),
        P(dp, "core", None),
        P(dp, "core", None),
        P(),
        P(),
        P(None, "core"),
        P(None, dp, "core"),
        P("core", dp),
        P(dp, "core"),
        P(None, dp, "core"),
        P("core", dp),
        P(dp, "core"),
        P("core"),
        P("core", dp),
    )
    return jax.shard_map(
        per_device,
        mesh=parts,
        in_specs=in_specs,
        out_specs=out_specs,
        check_vma=False,
    )
```

time: 946 us -> 700 us (0.74)
  waiting for transfers between devices: 475 us -> 212 us
  starting transfers between devices: 60.7 us -> 105 us
  other arithmetic: 103 us -> 64.3 us
  local copies, waits for them, and re-layouts: 69.7 us -> 87.2 us
  between operations: 16.1 us -> 4.09 us
    psum x1 -> x0, waiting for transfers between devices: 115 us -> none  [per_device(): lax.psum(jnp.concatenate([small.reshape(-1), head_place.reshape(-1), bias...]
    ppermute x24 -> x0, waiting for transfers between devices: 104 us -> none  [the longest x12 93.3 us: scatter_line(): lax.ppermute(block, axis, [(at, (at + step) % size) for at in range(size)])]
    ppermute x36 -> x95, starting transfers between devices: 27.4 us -> 105 us  [swap(): return lax.ppermute(values, axis, [(0, 1), (1, 0)])]
    ppermute x36 -> x95, waiting for transfers between devices: 255 us -> 212 us  [swap(): return lax.ppermute(values, axis, [(0, 1), (1, 0)])]
    ppermute x24 -> x0, starting transfers between devices: 33.3 us -> none  [the longest x12 18.7 us: gather_line(): lax.ppermute(block, axis, [(at, (at + step) % size) for at in range(size)])]
    dynamic_update_slice x13 -> x69, local copies, waits for them, and re-layouts: 12.6 us -> 33.5 us  [the longest x54 17.2 us: assemble(): whole = lax.dynamic_update_slice(whole, block, start)]
    concatenate x10 -> x3, other arithmetic: 13.6 us -> 0.03 us  [the longest x1 0.02 us: per_device(): jnp.concatenate([short(cross_kv[0]), short(cross_kv[1]), short(cross_out)...]
    another operation x17 -> x6, other arithmetic: 14.4 us -> 2.68 us  [the longest x12 10.8 us: gather_pair(): return jnp.stack(in_order(own, other, lax.axis_index(axis), dim), dim)]
  transfers between devices with their start and end apart: 61 -> 95, of which waited for: 23 -> 34; matrix products, arithmetic and copies ran while one was open for 26% -> 31% of each run, Pallas kernels for 10% -> 14%
where the time goes in v2:
time: 700 us; the launch traced here: 691 us
  waiting for transfers between devices  212 us (30%)
  Pallas kernels  117 us (17%)
  starting transfers between devices  105 us (15%)
  matrix products  101 us (14%)
  local copies, waits for them, and re-layouts  87.2 us (12%)
  other arithmetic  64.3 us (9%)
    ppermute x95, waiting for transfers between devices, swap(): return lax.ppermute(values, axis, [(0, 1), (1, 0)])  212 us
    ppermute x95, starting transfers between devices, swap(): return lax.ppermute(values, axis, [(0, 1), (1, 0)])  105 us
    dot_general x28, matrix products, dot(): lax.dot_general(left, right, (((left_dim,), (right_dim,)), ((), ())), pre...  101 us
    pallas_call x2, Pallas kernels, attend_back(): pl.pallas_call(functools.partial(backward_kernel, causal, tile, columns),...  51.3 us
    pallas_call x2, Pallas kernels, hidden_parts(): pl.pallas_call(functools.partial(hidden_kernel, min(256, rows)), grid=(hi...  37 us
    pallas_call x2, Pallas kernels, attend(): pl.pallas_call(functools.partial(forward_kernel, causal, tile), grid=(fea...  28.6 us
    dynamic_update_slice x54, local copies, waits for them, and re-layouts, assemble(): whole = lax.dynamic_update_slice(whole, block, start)  17.2 us
    unnamed x213, local copies, waits for them, and re-layouts  16.2 us
  transfers between devices with their start and end apart: 95, of which 34 were waited for; matrix products, arithmetic and copies ran while one was open for 31% of the time, Pallas kernels for 14%

profile of v2, /device:TPU:0, one launch (start us, length us, event | category | flops | bytes accessed | tf_op | source)
XLA Modules:
  0.0 690.7 jit_solution(9259795377803101066)
XLA Ops:
  24.0 7.7 %collective-permute-done.2 = bf16[1,1,1,1,64,1024]{5,4,3,2,1,0:T(8,128)(2,1)S(1)} collective-permute-done((bf16[1,1,1,1,64,1024]{5,4,3,2,1,0:T(8,128)(2,1)S(1)}, bf16[1,1,1,1,64,1024]{5,4,3,2,1,0:T(8,128)(2,1)S(1)}, u32[]{:S(2)}, u32[]{:S(2)}) %collective-permute-start.2) | collective-permute-done | bytes 131104 | tf_op jit(solution)/shard_map/ppermute | solution.py:42
  36.3 10.7 %collective-permute-done.7 = bf16[1,1,1,1,64,1536]{5,4,3,2,1,0:T(8,128)(2,1)S(1)} collective-permute-done((bf16[1,1,1,1,64,1536]{5,4,3,2,1,0:T(8,128)(2,1)S(1)}, bf16[1,1,1,1,64,1536]{5,4,3,2,1,0:T(8,128)(2,1)S(1)}, u32[]{:S(2)}, u32[]{:S(2)}) %collective-permute-start.7) | collective-permute-done | bytes 196640 | tf_op jit(solution)/shard_map/ppermute | solution.py:42
  51.8 6.9 collective-permute-start.12
  88.3 7.3 %collective-permute-done.15 = bf16[1,1,1,1,128,1024]{5,4,3,2,1,0:T(8,128)(2,1)S(1)} collective-permute-done((bf16[1,1,1,1,128,1024]{5,4,3,2,1,0:T(8,128)(2,1)S(1)}, bf16[1,1,1,1,128,1024]{5,4,3,2,1,0:T(8,128)(2,1)S(1)}, u32[]{:S(2)}, u32[]{:S(2)}) %collective-permute-start.15) | collective-permute-done | bytes 262176 | tf_op jit(solution)/shard_map/ppermute | solution.py:42
  99.3 15.6 %shard_map.263 = (bf16[1024,512]{1,0:T(8,128)(2,1)}, f32[4,2,1024]{2,1,0:T(2,128)}) custom-call(bf16[1024,1536]{1,0:T(8,128)(2,1)} %add_convert_fusion.q_ref.k_ref.v_ref, bf16[1024,1536]{1,0:T(8,128)(2,1)} %add_convert_fusion.q_ref.k_ref.v_ref, bf16[1024,1536]{1,0:T(8,128)(2,1)} %add_convert_fusion.q_ref.k_ref.v_ref, s32[1024,1]{1,0:T(8,128)} %copy.53.row_ref.col_ref, ...), custom_call_target="tpu_custom_call" | custom-call | flops 1024 | bytes 1024 | tf_op jit(solution)/shard_map/pallas_call | solution.py:286
  146.9 8.3 %collective-permute-done.23 = bf16[1,1,1,1,128,1024]{5,4,3,2,1,0:T(8,128)(2,1)S(1)} collective-permute-done((bf16[1,1,1,1,128,1024]{5,4,3,2,1,0:T(8,128)(2,1)S(1)}, bf16[1,1,1,1,128,1024]{5,4,3,2,1,0:T(8,128)(2,1)S(1)}, u32[]{:S(2)}, u32[]{:S(2)}) %collective-permute-start.23) | collective-permute-done | bytes 262176 | tf_op jit(solution)/shard_map/ppermute | solution.py:42
  160.3 10.9 %collective-permute-done.26 = bf16[2,2,2,1,64,1536]{5,4,3,2,1,0:T(8,128)(2,1)S(1)} collective-permute-done((bf16[2,2,2,1,64,1536]{5,4,3,2,1,0:T(8,128)(2,1)}, bf16[2,2,2,1,64,1536]{5,4,3,2,1,0:T(8,128)(2,1)S(1)}, u32[]{:S(2)}, u32[]{:S(2)}) %collective-permute-start.26) | collective-permute-done | bytes 1572896 | tf_op jit(solution)/shard_map/ppermute | solution.py:42
  176.8 8.1 %collective-permute-done.27 = bf16[1,1,1,1,128,1024]{5,4,2,1,0,3:T(8,128)(2,1)S(1)} collective-permute-done((bf16[1,1,1,1,128,1024]{5,4,2,1,0,3:T(8,128)(2,1)S(1)}, bf16[1,1,1,1,128,1024]{5,4,2,1,0,3:T(8,128)(2,1)S(1)}, u32[]{:S(2)}, u32[]{:S(2)}) %collective-permute-start.27) | collective-permute-done | bytes 262176 | tf_op jit(solution)/shard_map/ppermute | solution.py:42
  185.5 12.9 %shard_map.264 = (bf16[1024,512]{1,0:T(8,128)(2,1)}, f32[4,2,1024]{2,1,0:T(2,128)}) custom-call(bf16[1024,512]{1,0:T(8,128)(2,1)} %add_convert_fusion.10.q_ref, bf16[512,1024]{1,0:T(8,128)(2,1)} %add_convert_fusion.9.k_ref.v_ref, bf16[512,1024]{1,0:T(8,128)(2,1)} %add_convert_fusion.9.k_ref.v_ref, s32[1024,1]{1,0:T(8,128)} %copy.53.row_ref.col_ref, ...), custom_call_target="tpu_custom_call" | custom-call | flops 1024 | bytes 1024 | tf_op jit(solution)/shard_map/pallas_call | solution.py:286
  217.5 15.9 %collective-permute-done.32 = bf16[512,1024]{1,0:T(8,128)(2,1)} collective-permute-done((bf16[512,1024]{1,0:T(8,128)(2,1)S(1)}, bf16[512,1024]{1,0:T(8,128)(2,1)}, u32[]{:S(2)}, u32[]{:S(2)}) %collective-permute-start.32) | collective-permute-done | bytes 1048608 | tf_op jit(solution)/shard_map/ppermute | solution.py:42
  239.4 18.3 %collective-permute-done.36 = bf16[2,2,1,1,128,1024]{5,4,2,1,0,3:T(8,128)(2,1)S(1)} collective-permute-done((bf16[2,2,1,1,128,1024]{5,4,2,1,0,3:T(8,128)(2,1)S(1)}, bf16[2,2,1,1,128,1024]{5,4,2,1,0,3:T(8,128)(2,1)S(1)}, u32[]{:S(2)}, u32[]{:S(2)}) %collective-permute-start.36) | collective-permute-done | bytes 1048608 | tf_op jit(solution)/shard_map/ppermute | solution.py:42
  261.2 18.4 %shard_map.265 = (bf16[1024,2048]{1,0:T(8,128)(2,1)}, bf16[1024,2048]{1,0:T(8,128)(2,1)}) custom-call(bf16[1024,1024]{1,0:T(8,128)(2,1)} %constant_dynamic-update-slice_fusion.16.x_ref, bf16[1024,1024]{1,0:T(8,128)(2,1)} %copy-done.15, bf16[1024,2048]{1,0:T(8,128)(2,1)} %bitcast.419, bf16[1024,2048]{1,0:T(8,128)(2,1)} %bitcast.423, f32[1,2048]{1,0:T(1,128)} %bitcast.487), custom_call_target="tpu_custom_call" | custom-call | flops 1024 | bytes 1024 | tf_op jit(solution)/shard_map/pallas_call | solution.py:362
  279.6 8.0 %convolution_convert_fusion.5 = bf16[1024,1024]{1,0:T(8,128)(2,1)S(1)} fusion(bf16[1024,2048]{1,0:T(8,128)(2,1)} %get-tuple-element.148, bf16[1024,2048]{1,0:T(8,128)(2,1)} %bitcast.420), kind=kOutput, calls=%fused_computation.82 | convolution fusion | flops 4296015872 | bytes 10485760 | tf_op jit(solution)/shard_map/dot_general | solution.py:21
  304.3 18.6 %shard_map.266 = (bf16[1024,2048]{1,0:T(8,128)(2,1)}, bf16[1024,2048]{1,0:T(8,128)(2,1)}) custom-call(bf16[1024,1024]{1,0:T(8,128)(2,1)} %constant_dynamic-update-slice_fusion.2.x_ref, bf16[1024,1024]{1,0:T(8,128)(2,1)} %copy-done.17, bf16[1024,2048]{1,0:T(8,128)(2,1)} %bitcast.421, bf16[1024,2048]{1,0:T(8,128)(2,1)} %bitcast.424, f32[1,2048]{1,0:T(1,128)} %bitcast.488), custom_call_target="tpu_custom_call" | custom-call | flops 1024 | bytes 1024 | tf_op jit(solution)/shard_map/pallas_call | solution.py:362
  352.2 7.3 %collective-permute-done.41 = bf16[2,2,128,1024]{3,2,1,0:T(8,128)(2,1)S(1)} collective-permute-done((bf16[2,2,128,1024]{3,2,1,0:T(8,128)(2,1)S(1)}, bf16[2,2,128,1024]{3,2,1,0:T(8,128)(2,1)S(1)}, u32[]{:S(2)}, u32[]{:S(2)}) %collective-permute-start.41) | collective-permute-done | bytes 1048608 | tf_op jit(solution)/shard_map/ppermute | solution.py:42
  369.0 12.1 %collective-permute-done.42 = bf16[2,2,128,1024]{3,2,1,0:T(8,128)(2,1)S(1)} collective-permute-done((bf16[2,2,128,1024]{3,2,1,0:T(8,128)(2,1)S(1)}, bf16[2,2,128,1024]{3,2,1,0:T(8,128)(2,1)S(1)}, u32[]{:S(2)}, u32[]{:S(2)}) %collective-permute-start.42) | collective-permute-done | bytes 1048608 | tf_op jit(solution)/shard_map/ppermute | solution.py:42
  402.2 7.1 %fusion.111 = bf16[1024,1024]{1,0:T(8,128)(2,1)S(1)} fusion(bf16[1024,2048]{1,0:T(8,128)(2,1)} %get-tuple-element.164, bf16[1024,2048]{1,0:T(8,128)(2,1)S(1)} %bitcast.426), kind=kOutput, calls=%fused_computation.378 | convolution fusion | flops 4294967296 | bytes 10485760 | tf_op jit(solution)/shard_map/dot_general | solution.py:21
  409.3 9.7 %collective-permute-done.46 = bf16[512,1024]{1,0:T(8,128)(2,1)S(1)} collective-permute-done((bf16[512,1024]{1,0:T(8,128)(2,1)S(1)}, bf16[512,1024]{1,0:T(8,128)(2,1)S(1)}, u32[]{:S(2)}, u32[]{:S(2)}) %collective-permute-start.46) | collective-permute-done | bytes 1048608 | tf_op jit(solution)/shard_map/ppermute | solution.py:42
  433.7 10.3 %collective-permute-done.50 = bf16[2,128,1024]{2,1,0:T(8,128)(2,1)S(1)} collective-permute-done((bf16[2,128,1024]{2,1,0:T(8,128)(2,1)S(1)}, bf16[2,128,1024]{2,1,0:T(8,128)(2,1)S(1)}, u32[]{:S(2)}, u32[]{:S(2)}) %collective-permute-start.50) | collective-permute-done | bytes 524320 | tf_op jit(solution)/shard_map/ppermute | solution.py:42
  451.2 22.5 %shard_map.267 = (bf16[1024,512]{1,0:T(8,128)(2,1)}, bf16[512,1024]{1,0:T(8,128)(2,1)}) custom-call(bf16[1024,512]{1,0:T(8,128)(2,1)} %add_convert_fusion.10.q_ref, bf16[512,1024]{1,0:T(8,128)(2,1)} %add_convert_fusion.9.k_ref.v_ref, bf16[512,1024]{1,0:T(8,128)(2,1)} %add_convert_fusion.9.k_ref.v_ref, bf16[1024,512]{1,0:T(8,128)(2,1)} %get-tuple-element.141.o_ref, ...), custom_call_target="tpu_custom_call" | custom-call | flops 1024 | bytes 1024 | tf_op jit(solution)/shard_map/pallas_call | solution.py:314
  518.0 13.2 %collective-permute-done.59 = bf16[2,2,2,64,1024]{4,3,0,1,2:T(8,128)(2,1)S(1)} collective-permute-done((bf16[2,2,2,64,1024]{4,3,0,1,2:T(8,128)(2,1)S(1)}, bf16[2,2,2,64,1024]{4,3,0,1,2:T(8,128)(2,1)S(1)}, u32[]{:S(2)}, u32[]{:S(2)}) %collective-permute-start.59) | collective-permute-done | bytes 1048608 | tf_op jit(solution)/shard_map/ppermute | solution.py:42
  541.2 28.8 %shard_map.268 = bf16[1024,1536]{1,0:T(8,128)(2,1)} custom-call(bf16[1024,1536]{1,0:T(8,128)(2,1)} %add_convert_fusion.q_ref.k_ref.v_ref, bf16[1024,1536]{1,0:T(8,128)(2,1)} %add_convert_fusion.q_ref.k_ref.v_ref, bf16[1024,1536]{1,0:T(8,128)(2,1)} %add_convert_fusion.q_ref.k_ref.v_ref, bf16[1024,512]{1,0:T(8,128)(2,1)} %get-tuple-element.126.o_ref, ...), custom_call_target="tpu_custom_call" | custom-call | flops 1024 | bytes 1024 | tf_op jit(solution)/shard_map/pallas_call | solution.py:314
  581.9 9.4 %collective-permute-done.90 = bf16[64,1024]{1,0:T(8,128)(2,1)S(1)} collective-permute-done((bf16[64,1024]{1,0:T(8,128)(2,1)S(1)}, bf16[64,1024]{1,0:T(8,128)(2,1)S(1)}, u32[]{:S(2)}, u32[]{:S(2)}) %collective-permute-start.90) | collective-permute-done | bytes 131104 | tf_op jit(solution)/shard_map/ppermute | solution.py:42
  612.2 17.2 %collective-permute-done.65 = bf16[2,2,64,512]{3,2,0,1:T(8,128)(2,1)S(1)} collective-permute-done((bf16[2,2,64,512]{3,2,0,1:T(8,128)(2,1)S(1)}, bf16[2,2,64,512]{3,2,0,1:T(8,128)(2,1)S(1)}, u32[]{:S(2)}, u32[]{:S(2)}) %collective-permute-start.65) | collective-permute-done | bytes 262176 | tf_op jit(solution)/shard_map/ppermute | solution.py:42
  (711 shorter events, 381.3 us)
Async XLA Ops:
  9.4 61.5 %collective-permute-start = (bf16[512,1024]{1,0:T(8,128)(2,1)}, bf16[512,1024]{1,0:T(8,128)(2,1)}, u32[]{:S(2)}, u32[]{:S(2)}) collective-permute-start(bf16[512,1024]{1,0:T(8,128)(2,1)} %bitcast.471), channel_id=1, source_target_pairs={{0,1},{1,0},{2,3},{3,2},{4,5},{5,4},{6,7},{7,6},{8,9},{9,8},{10,11... | collective-permute-start | bytes 3145736 | tf_op jit(solution)/shard_map/ppermute | solution.py:42
  63.9 31.7 %collective-permute-start.16 = (bf16[2,2,1,1,64,1536]{5,4,3,2,1,0:T(8,128)(2,1)S(1)}, bf16[2,2,1,1,64,1536]{5,4,3,2,1,0:T(8,128)(2,1)S(1)}, u32[]{:S(2)}, u32[]{:S(2)}) collective-permute-start(bf16[2,2,1,1,64,1536]{5,4,3,2,1,0:T(8,128)(2,1)S(1)} %constant_dynamic-update-slice_fusion.42), channel_id=1, source_target_pairs={{0,4},{4,0},{1,5},{5,1},{2,6},{6,2},{3,7},{7,3},{8,12},{12,8},{9,1... | collective-permute-start | bytes 2359304 | tf_op jit(solution)/shard_map/ppermute | solution.py:42
  80.8 35.7 %collective-permute-start.19 = (bf16[2,2,2,1,64,1024]{5,4,3,2,1,0:T(8,128)(2,1)S(1)}, bf16[2,2,2,1,64,1024]{5,4,3,2,1,0:T(8,128)(2,1)}, u32[]{:S(2)}, u32[]{:S(2)}) collective-permute-start(bf16[2,2,2,1,64,1024]{5,4,3,2,1,0:T(8,128)(2,1)S(1)} %constant_dynamic-update-slice_fusion.52), channel_id=1, source_target_pairs={{0,2},{2,0},{1,3},{3,1},{4,6},{6,4},{5,7},{7,5},{8,10},{10,8},{9,1... | collective-permute-start | bytes 3145736 | tf_op jit(solution)/shard_map/ppermute | solution.py:42
  135.0 36.2 %collective-permute-start.26 = (bf16[2,2,2,1,64,1536]{5,4,3,2,1,0:T(8,128)(2,1)}, bf16[2,2,2,1,64,1536]{5,4,3,2,1,0:T(8,128)(2,1)S(1)}, u32[]{:S(2)}, u32[]{:S(2)}) collective-permute-start(bf16[2,2,2,1,64,1536]{5,4,3,2,1,0:T(8,128)(2,1)} %constant_dynamic-update-slice_fusion.35), channel_id=1, source_target_pairs={{0,2},{2,0},{1,3},{3,1},{4,6},{6,4},{5,7},{7,5},{8,10},{10,8},{9,1... | collective-permute-start | bytes 4718600 | tf_op jit(solution)/shard_map/ppermute | solution.py:42
  140.7 44.7 %collective-permute-start.28 = (bf16[2,2,1,1,128,1024]{5,4,2,1,0,3:T(8,128)(2,1)S(1)}, bf16[2,2,1,1,128,1024]{5,4,2,1,0,3:T(8,128)(2,1)}, u32[]{:S(2)}, u32[]{:S(2)}) collective-permute-start(bf16[2,2,1,1,128,1024]{5,4,2,1,0,3:T(8,128)(2,1)S(1)} %constant_dynamic-update-slice_fusion.33), channel_id=1, source_target_pairs={{0,4},{4,0},{1,5},{5,1},{2,6},{6,2},{3,7},{7,3},{8,12},{12,8},{9,1... | collective-permute-start | bytes 3145736 | tf_op jit(solution)/shard_map/ppermute | solution.py:42
  158.0 40.7 %collective-permute-start.30 = (bf16[2,2,1,1,128,1024]{5,4,2,1,0,3:T(8,128)(2,1)S(1)}, bf16[2,2,1,1,128,1024]{5,4,2,1,0,3:T(8,128)(2,1)}, u32[]{:S(2)}, u32[]{:S(2)}) collective-permute-start(bf16[2,2,1,1,128,1024]{5,4,2,1,0,3:T(8,128)(2,1)S(1)} %constant_dynamic-update-slice_fusion.29), channel_id=1, source_target_pairs={{0,4},{4,0},{1,5},{5,1},{2,6},{6,2},{3,7},{7,3},{8,12},{12,8},{9,1... | collective-permute-start | bytes 3145736 | tf_op jit(solution)/shard_map/ppermute | solution.py:42
  209.8 48.0 %collective-permute-start.35 = (bf16[2,2,1,1,128,1024]{5,4,2,1,0,3:T(8,128)(2,1)S(1)}, bf16[2,2,1,1,128,1024]{5,4,2,1,0,3:T(8,128)(2,1)S(1)}, u32[]{:S(2)}, u32[]{:S(2)}) collective-permute-start(bf16[2,2,1,1,128,1024]{5,4,2,1,0,3:T(8,128)(2,1)S(1)} %copy-done.24), channel_id=1, source_target_pairs={{0,4},{4,0},{1,5},{5,1},{2,6},{6,2},{3,7},{7,3},{8,12},{12,8},{9,1... | collective-permute-start | bytes 3145736 | tf_op jit(solution)/shard_map/ppermute | solution.py:42
  209.8 48.0 %collective-permute-start.36 = (bf16[2,2,1,1,128,1024]{5,4,2,1,0,3:T(8,128)(2,1)S(1)}, bf16[2,2,1,1,128,1024]{5,4,2,1,0,3:T(8,128)(2,1)S(1)}, u32[]{:S(2)}, u32[]{:S(2)}) collective-permute-start(bf16[2,2,1,1,128,1024]{5,4,2,1,0,3:T(8,128)(2,1)S(1)} %copy-done.26), channel_id=1, source_target_pairs={{0,4},{4,0},{1,5},{5,1},{2,6},{6,2},{3,7},{7,3},{8,12},{12,8},{9,1... | collective-permute-start | bytes 3145736 | tf_op jit(solution)/shard_map/ppermute | solution.py:42
  236.5 54.6 %collective-permute-start.38 = (bf16[512,1024]{1,0:T(8,128)(2,1)}, bf16[512,1024]{1,0:T(8,128)(2,1)}, u32[]{:S(2)}, u32[]{:S(2)}) collective-permute-start(bf16[512,1024]{1,0:T(8,128)(2,1)} %collective-permute-done.32), channel_id=1, source_target_pairs={{0,1},{1,0},{2,3},{3,2},{4,5},{5,4},{6,7},{7,6},{8,9},{9,8},{10,11... | collective-permute-start | bytes 3145736 | tf_op jit(solution)/shard_map/ppermute | solution.py:42
  238.4 52.2 %collective-permute-start.39 = (bf16[512,1024]{1,0:T(8,128)(2,1)}, bf16[512,1024]{1,0:T(8,128)(2,1)}, u32[]{:S(2)}, u32[]{:S(2)}) collective-permute-start(bf16[512,1024]{1,0:T(8,128)(2,1)} %get-tuple-element.143), channel_id=1, source_target_pairs={{0,2},{2,0},{1,3},{3,1},{4,6},{6,4},{5,7},{7,5},{8,10},{10,8},{9,1... | collective-permute-start | bytes 3145736 | tf_op jit(solution)/shard_map/ppermute | solution.py:42
  334.6 46.4 %collective-permute-start.42 = (bf16[2,2,128,1024]{3,2,1,0:T(8,128)(2,1)S(1)}, bf16[2,2,128,1024]{3,2,1,0:T(8,128)(2,1)S(1)}, u32[]{:S(2)}, u32[]{:S(2)}) collective-permute-start(bf16[2,2,128,1024]{3,2,1,0:T(8,128)(2,1)S(1)} %dynamic-slice_bitcast_fusion.6), channel_id=1, source_target_pairs={{0,4},{4,0},{1,5},{5,1},{2,6},{6,2},{3,7},{7,3},{8,12},{12,8},{9,1... | collective-permute-start | bytes 3145736 | tf_op jit(solution)/shard_map/ppermute | solution.py:42
  342.7 48.6 %collective-permute-start.45 = (bf16[512,1024]{1,0:T(8,128)(2,1)}, bf16[512,1024]{1,0:T(8,128)(2,1)}, u32[]{:S(2)}, u32[]{:S(2)}) collective-permute-start(bf16[512,1024]{1,0:T(8,128)(2,1)} %dynamic-slice_bitcast_fusion.3), channel_id=1, source_target_pairs={{0,1},{1,0},{2,3},{3,2},{4,5},{5,4},{6,7},{7,6},{8,9},{9,8},{10,11... | collective-permute-start | bytes 3145736 | tf_op jit(solution)/shard_map/ppermute | solution.py:42
  396.4 36.9 %collective-permute-start.51 = (bf16[2,2,128,1024]{3,2,1,0:T(8,128)(2,1)S(1)}, bf16[2,2,128,1024]{3,2,1,0:T(8,128)(2,1)S(1)}, u32[]{:S(2)}, u32[]{:S(2)}) collective-permute-start(bf16[2,2,128,1024]{3,2,1,0:T(8,128)(2,1)S(1)} %dynamic-slice_bitcast_fusion.2), channel_id=1, source_target_pairs={{0,4},{4,0},{1,5},{5,1},{2,6},{6,2},{3,7},{7,3},{8,12},{12,8},{9,1... | collective-permute-start | bytes 3145736 | tf_op jit(solution)/shard_map/ppermute | solution.py:42
  397.8 83.8 %collective-permute-start.54 = (bf16[2,2,128,1024]{3,2,1,0:T(8,128)(2,1)}, bf16[2,2,128,1024]{3,2,1,0:T(8,128)(2,1)}, u32[]{:S(2)}, u32[]{:S(2)}) collective-permute-start(bf16[2,2,128,1024]{3,2,1,0:T(8,128)(2,1)} %dynamic-slice_bitcast_fusion.1), channel_id=1, source_target_pairs={{0,4},{4,0},{1,5},{5,1},{2,6},{6,2},{3,7},{7,3},{8,12},{12,8},{9,1... | collective-permute-start | bytes 3145736 | tf_op jit(solution)/shard_map/ppermute | solution.py:42
  428.9 176.6 %collective-permute-start.47 = (bf16[512,1024]{1,0:T(8,128)(2,1)}, bf16[512,1024]{1,0:T(8,128)(2,1)}, u32[]{:S(2)}, u32[]{:S(2)}) collective-permute-start(bf16[512,1024]{1,0:T(8,128)(2,1)} %convert_add_fusion.9), channel_id=1, source_target_pairs={{0,2},{2,0},{1,3},{3,1},{4,6},{6,4},{5,7},{7,5},{8,10},{10,8},{9,1... | collective-permute-start | bytes 3145736 | tf_op jit(solution)/shard_map/ppermute | solution.py:42
  446.6 37.2 %collective-permute-start.92 = (bf16[128,1024]{1,0:T(8,128)(2,1)S(1)}, bf16[128,1024]{1,0:T(8,128)(2,1)}, u32[]{:S(2)}, u32[]{:S(2)}) collective-permute-start(bf16[128,1024]{1,0:T(8,128)(2,1)S(1)} %dynamic-slice_bitcast_fusion.18), channel_id=1, source_target_pairs={{0,16},{16,0},{1,17},{17,1},{2,18},{18,2},{3,19},{19,3},{4,20},{20... | collective-permute-start | bytes 786440 | tf_op jit(solution)/shard_map/ppermute | solution.py:42
  448.5 37.9 %collective-permute-start.93 = (bf16[64,1024]{1,0:T(8,128)(2,1)S(1)}, bf16[64,1024]{1,0:T(8,128)(2,1)}, u32[]{:S(2)}, u32[]{:S(2)}) collective-permute-start(bf16[64,1024]{1,0:T(8,128)(2,1)S(1)} %fusion.84), channel_id=1, source_target_pairs={{0,2},{2,0},{1,3},{3,1},{4,6},{6,4},{5,7},{7,5},{8,10},{10,8},{9,1... | collective-permute-start | bytes 393224 | tf_op jit(solution)/shard_map/ppermute | solution.py:42
  449.6 44.1 %collective-permute-start.58 = (bf16[2,128,1024]{2,1,0:T(8,128)(2,1)}, bf16[2,128,1024]{2,1,0:T(8,128)(2,1)}, u32[]{:S(2)}, u32[]{:S(2)}) collective-permute-start(bf16[2,128,1024]{2,1,0:T(8,128)(2,1)} %dynamic-slice_bitcast_fusion.11), channel_id=1, source_target_pairs={{0,8},{8,0},{1,9},{9,1},{2,10},{10,2},{3,11},{11,3},{4,12},{12,4},... | collective-permute-start | bytes 1572872 | tf_op jit(solution)/shard_map/ppermute | solution.py:42
  491.4 41.0 %collective-permute-start.55 = (bf16[2,128,1024]{2,1,0:T(8,128)(2,1)S(1)}, bf16[2,128,1024]{2,1,0:T(8,128)(2,1)S(1)}, u32[]{:S(2)}, u32[]{:S(2)}) collective-permute-start(bf16[2,128,1024]{2,1,0:T(8,128)(2,1)S(1)} %dynamic-slice_bitcast_fusion.12), channel_id=1, source_target_pairs={{0,8},{8,0},{1,9},{9,1},{2,10},{10,2},{3,11},{11,3},{4,12},{12,4},... | collective-permute-start | bytes 1572872 | tf_op jit(solution)/shard_map/ppermute | solution.py:42
  534.5 44.8 %collective-permute-start.88 = (bf16[128,1024]{1,0:T(8,128)(2,1)}, bf16[128,1024]{1,0:T(8,128)(2,1)}, u32[]{:S(2)}, u32[]{:S(2)}) collective-permute-start(bf16[128,1024]{1,0:T(8,128)(2,1)} %dynamic-slice_bitcast_fusion.22), channel_id=1, source_target_pairs={{0,16},{16,0},{1,17},{17,1},{2,18},{18,2},{3,19},{19,3},{4,20},{20... | collective-permute-start | bytes 786440 | tf_op jit(solution)/shard_map/ppermute | solution.py:42
  535.9 46.0 %collective-permute-start.89 = (bf16[64,1024]{1,0:T(8,128)(2,1)S(1)}, bf16[64,1024]{1,0:T(8,128)(2,1)}, u32[]{:S(2)}, u32[]{:S(2)}) collective-permute-start(bf16[64,1024]{1,0:T(8,128)(2,1)S(1)} %fusion.82), channel_id=1, source_target_pairs={{0,2},{2,0},{1,3},{3,1},{4,6},{6,4},{5,7},{7,5},{8,10},{10,8},{9,1... | collective-permute-start | bytes 393224 | tf_op jit(solution)/shard_map/ppermute | solution.py:42
  537.1 40.1 %collective-permute-start.85 = (bf16[2,64,512]{2,1,0:T(8,128)(2,1)}, bf16[2,64,512]{2,1,0:T(8,128)(2,1)}, u32[]{:S(2)}, u32[]{:S(2)}) collective-permute-start(bf16[2,64,512]{2,1,0:T(8,128)(2,1)} %dynamic-slice_bitcast_fusion.32), channel_id=1, source_target_pairs={{0,8},{8,0},{1,9},{9,1},{2,10},{10,2},{3,11},{11,3},{4,12},{12,4},... | collective-permute-start | bytes 393224 | tf_op jit(solution)/shard_map/ppermute | solution.py:42
  540.2 52.4 %collective-permute-start.60 = (bf16[2,2,2,64,512]{4,3,0,1,2:T(8,128)(2,1)}, bf16[2,2,2,64,512]{4,3,0,1,2:T(8,128)(2,1)}, u32[]{:S(2)}, u32[]{:S(2)}) collective-permute-start(bf16[2,2,2,64,512]{4,3,0,1,2:T(8,128)(2,1)} %bitcast.416), channel_id=1, source_target_pairs={{0,2},{2,0},{1,3},{3,1},{4,6},{6,4},{5,7},{7,5},{8,10},{10,8},{9,1... | collective-permute-start | bytes 1572872 | tf_op jit(solution)/shard_map/ppermute | solution.py:42
  592.6 49.8 %collective-permute-start.86 = (bf16[64,512]{1,0:T(8,128)(2,1)S(1)}, bf16[64,512]{1,0:T(8,128)(2,1)S(1)}, u32[]{:S(2)}, u32[]{:S(2)}) collective-permute-start(bf16[64,512]{1,0:T(8,128)(2,1)S(1)} %dynamic-slice_bitcast_fusion.38), channel_id=1, source_target_pairs={{0,16},{16,0},{1,17},{17,1},{2,18},{18,2},{3,19},{19,3},{4,20},{20... | collective-permute-start | bytes 196616 | tf_op jit(solution)/shard_map/ppermute | solution.py:42
  (177 other events, 1975.5 us)
